TPU v7x, 32 devices: a whole 2x2x4 slice. The times are simulated.
32 devices in a mesh: seq: 16 (over z, y, x), batch: 2 (over core).
Axes of the slice: x: 2, y: 2, z: 4, core: 2. Of those that a mesh axis runs over, the one named last changes fastest.
Arguments:
- inputs: bfloat16 [8, 2048, 512], P('batch', 'seq'), may hold values from -6 to 6
- out_grad: bfloat16 [8, 2048, 512], P('batch', 'seq'), may hold values from -6 to 6
- log_rate: float32 [512, 64], replicated, as said below
- pole_angle: float32 [512, 64], replicated, may hold values from -3.140625 to 3.140625
- weight_real: float32 [512, 64], replicated, may hold values from -0.75 to 0.75
- weight_imag: float32 [512, 64], replicated, may hold values from -0.75 to 0.75
- passthrough: float32 [512], replicated, may hold values from -4 to 4
Outputs:
- input_grad: bfloat16 [8, 2048, 512], P('batch', 'seq')
- rate_grad: float32 [512, 64], replicated
- angle_grad: float32 [512, 64], replicated
- weight_real_grad: float32 [512, 64], replicated
- weight_imag_grad: float32 [512, 64], replicated
- passthrough_grad: float32 [512], replicated
Inputs may be any that keep to these rules, and one draw needn't show every extreme that they name: `log_rate`: every entry lies between the natural logarithm of 0.0001 and the natural logarithm of 0.08.
All inputs are finite; a program needn't handle non-finite values.
Results may differ from a plain program's by a relative error of at most 0.0064.
Values may be sent and summed in bfloat16 or wider, within the bound.
A program may use at most 64 MiB of HBM per device.

v0:
```python
import math

import jax
import jax.numpy as jnp
from jax import lax
from jax.sharding import PartitionSpec as P

TWO_PI = 2.0 * math.pi
span_rows = 16


def cos_sin(numerator, length):
    phases = (numerator % length).astype(jnp.float32) * (TWO_PI / length)
    return (jnp.cos(phases), -jnp.sin(phases))


def spectrum_terms(parameters, z_real, z_imag):
    log_rate, pole_angle, weight_real, weight_imag = parameters
    log_rate = log_rate.T
    pole_angle = pole_angle.T
    weight_real = weight_real.T
    weight_imag = weight_imag.T
    rate = jnp.exp(log_rate)
    radius = jnp.exp(-rate)
    pole_real = radius * jnp.cos(pole_angle)
    pole_imag = radius * jnp.sin(pole_angle)
    shrink = jnp.sqrt(-jnp.expm1(-2.0 * rate))
    scaled_real = weight_real * shrink
    scaled_imag = weight_imag * shrink
    z_real = z_real[:, None, None]
    z_imag = z_imag[:, None, None]
    diff_real = z_real - pole_real
    diff_upper = z_imag - pole_imag
    diff_lower = z_imag + pole_imag
    inv_upper = 1.0 / (diff_real * diff_real + diff_upper * diff_upper)
    inv_lower = 1.0 / (diff_real * diff_real + diff_lower * diff_lower)
    part_real = (scaled_real * diff_real + scaled_imag * diff_upper) * inv_upper + (
        scaled_real * diff_real - scaled_imag * diff_lower
    ) * inv_lower
    part_imag = (scaled_imag * diff_real - scaled_real * diff_upper) * inv_upper - (
        scaled_imag * diff_real + scaled_real * diff_lower
    ) * inv_lower
    return (jnp.sum(part_real, axis=1), jnp.sum(part_imag, axis=1))


def matmul(form, left, right):
    return jnp.einsum(form, left, right, preferred_element_type=jnp.float32)


def local(inputs, out_grad, log_rate, pole_angle, weight_real, weight_imag, passthrough):
    parameters = (log_rate, pole_angle, weight_real, weight_imag)
    batch_rows, seq_len, channels = inputs.shape
    seq_devices = lax.axis_size("seq")
    member = lax.axis_index("seq")
    slice_len = seq_len // seq_devices
    freq_rows = 2 * seq_devices
    n_freq = freq_rows * seq_len
    row_index = jnp.arange(seq_devices, dtype=jnp.int32)
    col_index = jnp.arange(freq_rows, dtype=jnp.int32)
    positions = jnp.arange(seq_len, dtype=jnp.int32)
    cos_one, sin_one = cos_sin(row_index[:, None] * col_index[None, :], freq_rows)
    cos_one = cos_one.astype(jnp.bfloat16)
    sin_one = sin_one.astype(jnp.bfloat16)
    cos_two, sin_two = cos_sin(positions[:, None] * positions[None, :], seq_len)
    cos_two = cos_two.astype(jnp.bfloat16)
    sin_two = sin_two.astype(jnp.bfloat16)
    own_places = member * slice_len + jnp.arange(slice_len, dtype=jnp.int32)
    turn_real, turn_imag = cos_sin(own_places[:, None] * col_index[None, :], n_freq)
    turn_real = turn_real[None, :, :, None]
    turn_imag = turn_imag[None, :, :, None]
    own_freq = 2 * member + jnp.arange(2, dtype=jnp.int32)
    back_real_turn, back_imag_turn = cos_sin(positions[:, None] * own_freq[None, :], n_freq)
    back_real_turn = back_real_turn[None, :, :, None]
    back_imag_turn = back_imag_turn[None, :, :, None]

    def kernel_part(values, offset):
        spectral_rows = offset + jnp.arange(span_rows, dtype=jnp.int32)
        frequency = own_freq[None, :] + freq_rows * spectral_rows[:, None]
        phases = frequency.reshape(-1).astype(jnp.float32) * (TWO_PI / n_freq)
        part_real, part_imag = spectrum_terms(values, jnp.cos(phases), jnp.sin(phases))
        return (
            part_real.reshape(span_rows, 2, channels),
            part_imag.reshape(span_rows, 2, channels),
        )

    starts = jnp.arange(seq_len // span_rows, dtype=jnp.int32) * span_rows
    kern_real, kern_imag = lax.map(lambda offset: kernel_part(parameters, offset), starts)
    kern_real = kern_real.reshape(seq_len, 2, channels)
    kern_imag = kern_imag.reshape(seq_len, 2, channels)

    def section_one(blocks):
        part_real = matmul("brmc,rk->bmkc", blocks, cos_one)
        part_imag = matmul("brmc,rk->bmkc", blocks, sin_one)
        g_real = (part_real * turn_real - part_imag * turn_imag).astype(jnp.bfloat16)
        g_imag = (part_real * turn_imag + part_imag * turn_real).astype(jnp.bfloat16)
        return (g_real, g_imag)

    def section_two(g_real, g_imag):
        spec_real = matmul("bmjc,mq->bqjc", g_real, cos_two) - matmul(
            "bmjc,mq->bqjc", g_imag, sin_two
        )
        spec_imag = matmul("bmjc,mq->bqjc", g_real, sin_two) + matmul(
            "bmjc,mq->bqjc", g_imag, cos_two
        )
        return (spec_real, spec_imag)

    in_columns, grad_columns = (
        lax.all_to_all(inputs[:, None], "seq", split_axis=2, concat_axis=1, tiled=True),
        lax.all_to_all(out_grad[:, None], "seq", split_axis=2, concat_axis=1, tiled=True),
    )
    in_g_real, in_g_imag = section_one(in_columns)
    out_g_real, out_g_imag = section_one(grad_columns)
    in_s_real, in_s_imag, out_s_real, out_s_imag = (
        lax.all_to_all(in_g_real, "seq", split_axis=2, concat_axis=1, tiled=True),
        lax.all_to_all(in_g_imag, "seq", split_axis=2, concat_axis=1, tiled=True),
        lax.all_to_all(out_g_real, "seq", split_axis=2, concat_axis=1, tiled=True),
        lax.all_to_all(out_g_imag, "seq", split_axis=2, concat_axis=1, tiled=True),
    )
    in_real, in_imag = section_two(in_s_real, in_s_imag)
    out_real, out_imag = section_two(out_s_real, out_s_imag)
    prod_real = ((kern_real * out_real + kern_imag * out_imag) / n_freq).astype(jnp.bfloat16)
    prod_imag = ((kern_real * out_imag - kern_imag * out_real) / n_freq).astype(jnp.bfloat16)
    back_real = matmul("bqjc,qm->bmjc", prod_real, cos_two) + matmul(
        "bqjc,qm->bmjc", prod_imag, sin_two
    )
    back_imag = matmul("bqjc,qm->bmjc", prod_imag, cos_two) - matmul(
        "bqjc,qm->bmjc", prod_real, sin_two
    )
    turned_real = (back_real * back_real_turn + back_imag * back_imag_turn).astype(jnp.bfloat16)
    turned_imag = (back_imag * back_real_turn - back_real * back_imag_turn).astype(jnp.bfloat16)
    rows_real = lax.all_to_all(turned_real, "seq", split_axis=1, concat_axis=2, tiled=True)
    rows_imag = lax.all_to_all(turned_imag, "seq", split_axis=1, concat_axis=2, tiled=True)
    conv = matmul("bmkc,rk->brmc", rows_real, cos_one) + matmul("bmkc,rk->brmc", rows_imag, sin_one)
    conv = lax.all_to_all(conv.astype(jnp.bfloat16), "seq", split_axis=1, concat_axis=2, tiled=True)
    conv = conv.reshape(batch_rows, seq_len, channels)
    input_grad = (conv.astype(jnp.float32) + passthrough * out_grad.astype(jnp.float32)).astype(
        jnp.bfloat16
    )
    spec_real = jnp.sum(out_real * in_real + out_imag * in_imag, axis=0) / n_freq
    spec_imag = jnp.sum(out_real * in_imag - out_imag * in_real, axis=0) / n_freq
    anchor = 0

    def grad_step(running, offset):
        slab_real = lax.dynamic_slice_in_dim(spec_real, offset, span_rows, 0)
        slab_imag = lax.dynamic_slice_in_dim(spec_imag, offset, span_rows, 0)
        unused, pull = jax.vjp(lambda values: kernel_part(values, anchor + offset), parameters)
        pulled = pull((slab_real, -slab_imag))[0]
        return (tuple((left + right for left, right in zip(running, pulled))), None)

    grad_starts = jnp.arange(spec_real.shape[0] // span_rows, dtype=jnp.int32) * span_rows
    initial = tuple((jnp.zeros_like(values) for values in parameters))
    pulled, unused = lax.scan(grad_step, initial, grad_starts)
    passthrough_part = jnp.sum(
        inputs.astype(jnp.float32) * out_grad.astype(jnp.float32), axis=(0, 1)
    )
    summed = lax.psum(
        (pulled[0], pulled[1], pulled[2], pulled[3], passthrough_part), ("seq", "batch")
    )
    return (input_grad, summed[0], summed[1], summed[2], summed[3], summed[4])


def solution(mesh):
    placed = (P("batch", "seq", None), P("batch", "seq", None), P(), P(), P(), P(), P())
    return jax.shard_map(
        local,
        mesh=mesh,
        in_specs=placed,
        out_specs=(P("batch", "seq", None), P(), P(), P(), P(), P()),
        check_vma=False,
    )
```

profile of v0, /device:TPU:15, one launch (start us, length us, event | category | flops | bytes accessed | tf_op | source)
XLA Modules:
  0.0 568.6 jit_solution(4343227834854203855)
XLA Ops:
  9.5 6.6 %all-to-all-start = ((bf16[4,1,128,512]{3,0,1,2:T(4,128)(2,1)}), bf16[4,1,128,512]{3,0,1,2:T(4,128)(2,1)S(1)}, u32[]{:S(2)}, u32[]{:S(2)}) async-start(bf16[4,1,128,512]{3,0,1,2:T(4,128)(2,1)} %bitcast.253), calls=%async_computation | async-start | bytes 1048576 | tf_op jit(solution)/shard_map/all_to_all | solution.py:109
  17.3 11.3 %all-to-all-done = bf16[4,1,128,512]{3,0,1,2:T(4,128)(2,1)S(1)} async-done(((bf16[4,1,128,512]{3,0,1,2:T(4,128)(2,1)}), bf16[4,1,128,512]{3,0,1,2:T(4,128)(2,1)S(1)}, u32[]{:S(2)}, u32[]{:S(2)}) %all-to-all-start) | async-done | bytes 524320 | tf_op jit(solution)/shard_map/all_to_all | solution.py:109
  28.6 5.8 %all-to-all-start.6 = ((bf16[4,1,128,512]{3,0,1,2:T(4,128)(2,1)}), bf16[4,1,128,512]{3,0,1,2:T(4,128)(2,1)S(1)}, u32[]{:S(2)}, u32[]{:S(2)}) async-start(bf16[4,1,128,512]{3,0,1,2:T(4,128)(2,1)} %bitcast.251), calls=%async_computation.6 | async-start | bytes 1048576 | tf_op jit(solution)/shard_map/all_to_all | solution.py:108
  37.0 9.9 %all-to-all-done.6 = bf16[4,1,128,512]{3,0,1,2:T(4,128)(2,1)S(1)} async-done(((bf16[4,1,128,512]{3,0,1,2:T(4,128)(2,1)}), bf16[4,1,128,512]{3,0,1,2:T(4,128)(2,1)S(1)}, u32[]{:S(2)}, u32[]{:S(2)}) %all-to-all-start.6) | async-done | bytes 524320 | tf_op jit(solution)/shard_map/all_to_all | solution.py:108
  52.7 5.7 all-to-all-start.7
  60.0 22.3 %all-to-all-done.7 = bf16[4,8,32,512]{3,1,0,2:T(8,128)(2,1)S(1)} async-done(((bf16[4,8,32,512]{3,1,0,2:T(8,128)(2,1)}), bf16[4,8,32,512]{3,1,0,2:T(8,128)(2,1)S(1)}, u32[]{:S(2)}, u32[]{:S(2)}) %all-to-all-start.7) | async-done | bytes 1048608 | tf_op jit(solution)/shard_map/all_to_all | solution.py:114
  82.3 4.9 all-to-all-start.8
  90.6 20.4 %all-to-all-done.8 = bf16[4,8,32,512]{3,1,0,2:T(8,128)(2,1)S(1)} async-done(((bf16[4,8,32,512]{3,1,0,2:T(8,128)(2,1)}), bf16[4,8,32,512]{3,1,0,2:T(8,128)(2,1)S(1)}, u32[]{:S(2)}, u32[]{:S(2)}) %all-to-all-start.8) | async-done | bytes 1048608 | tf_op jit(solution)/shard_map/all_to_all | solution.py:115
  111.1 5.0 all-to-all-start.1
  116.1 53.9 %while.34 = (s32[]{:T(128)}, f32[8,16,2,512]{3,2,1,0:T(2,128)S(1)}, f32[8,16,2,512]{3,2,1,0:T(2,128)}, f32[512,64]{0,1:T(8,128)S(1)}, f32[64,512]{1,0:T(8,128)S(...) while((s32[]{:T(128)}, f32[8,16,2,512]{3,2,1,0:T(2,128)S(1)}, ...), condition=%wide.region_3.4_spmd.clone, body=%wide.region_0.3_spmd.clone.sunk | while | flops 29458564 | bytes 1836817 | solution.py:87
  117.7 4.3 fusion.262
  124.5 4.3 fusion.262
  131.2 4.3 fusion.262
  158.2 4.3 fusion.262
  173.0 6.5 %all-to-all-start.2 = ((bf16[4,8,32,512]{3,1,0,2:T(8,128)(2,1)}), bf16[4,8,32,512]{3,1,0,2:T(8,128)(2,1)}, u32[]{:S(2)}, u32[]{:S(2)}) async-start(bf16[4,8,32,512]{3,1,0,2:T(8,128)(2,1)} %copy.115), calls=%async_computation.2 | async-start | bytes 2097152 | tf_op jit(solution)/shard_map/all_to_all | solution.py:117
  192.1 11.3 %all-to-all-done.2 = bf16[4,8,32,512]{3,1,0,2:T(8,128)(2,1)} async-done(((bf16[4,8,32,512]{3,1,0,2:T(8,128)(2,1)}), bf16[4,8,32,512]{3,1,0,2:T(8,128)(2,1)}, u32[]{:S(2)}, u32[]{:S(2)}) %all-to-all-start.2) | async-done | bytes 1048608 | tf_op jit(solution)/shard_map/all_to_all | solution.py:117
  216.0 5.1 all-to-all-start.3
  223.2 21.8 %all-to-all-done.3 = bf16[4,128,2,512]{3,2,0,1:T(2,128)(2,1)S(1)} async-done(((bf16[4,128,2,512]{3,2,0,1:T(2,128)(2,1)}), bf16[4,128,2,512]{3,2,0,1:T(2,128)(2,1)S(1)}, u32[]{:S(2)}, u32[]{:S(2)}) %all-to-all-start.3) | async-done | bytes 1048608 | tf_op jit(solution)/shard_map/all_to_all | solution.py:131
  245.0 5.0 all-to-all-start.4
  258.5 15.7 %all-to-all-done.4 = bf16[4,128,2,512]{3,2,0,1:T(2,128)(2,1)} async-done(((bf16[4,128,2,512]{3,2,0,1:T(2,128)(2,1)}), bf16[4,128,2,512]{3,2,0,1:T(2,128)(2,1)}, u32[]{:S(2)}, u32[]{:S(2)}) %all-to-all-start.4) | async-done | bytes 1048608 | tf_op jit(solution)/shard_map/all_to_all | solution.py:132
  282.4 5.3 all-to-all-start.5
  287.7 138.0 %while.35 = (s32[]{:T(128)}, f32[512,64]{0,1:T(8,128)S(1)}, f32[512,64]{0,1:T(8,128)S(1)}, f32[512,64]{0,1:T(8,128)S(1)}, f32[512,64]{0,1:T(8,128)S(1)}, /*index...) while((s32[]{:T(128)}, f32[512,64]{0,1:T(8,128)S(1)}, ...), condition=%wide.region_18.19_spmd.clone, body=%wide.region_6.18_spmd.clone.sunk | while | flops 88277128 | bytes 7669130 | solution.py:152
  292.6 12.0 %fusion.264 = (f32[64,512]{1,0:T(8,128)S(1)}, f32[64,512]{1,0:T(8,128)S(1)}, f32[64,512]{1,0:T(8,128)S(1)}, f32[64,512]{1,0:T(8,128)S(1)}, f32[64,512]{1,0:T(8,1...) fusion(f32[64,512]{1,0:T(8,128)S(1)} %get-tuple-element.803, ...), kind=kLoop, calls=%fused_computation.79.clone.1 | loop fusion | flops 86671360 | bytes 2162944 | tf_op jit(solution)/shard_map/while/body/eval_jaxpr/transpose(jvp())/reduce_sum | solution.py:33
  309.8 12.0 %fusion.264 = (f32[64,512]{1,0:T(8,128)S(1)}, f32[64,512]{1,0:T(8,128)S(1)}, f32[64,512]{1,0:T(8,128)S(1)}, f32[64,512]{1,0:T(8,128)S(1)}, f32[64,512]{1,0:T(8,1...) fusion(f32[64,512]{1,0:T(8,128)S(1)} %get-tuple-element.803, ...), kind=kLoop, calls=%fused_computation.79.clone.1 | loop fusion | flops 86671360 | bytes 2162944 | tf_op jit(solution)/shard_map/while/body/eval_jaxpr/transpose(jvp())/reduce_sum | solution.py:33
  327.1 12.0 %fusion.264 = (f32[64,512]{1,0:T(8,128)S(1)}, f32[64,512]{1,0:T(8,128)S(1)}, f32[64,512]{1,0:T(8,128)S(1)}, f32[64,512]{1,0:T(8,128)S(1)}, f32[64,512]{1,0:T(8,1...) fusion(f32[64,512]{1,0:T(8,128)S(1)} %get-tuple-element.803, ...), kind=kLoop, calls=%fused_computation.79.clone.1 | loop fusion | flops 86671360 | bytes 2162944 | tf_op jit(solution)/shard_map/while/body/eval_jaxpr/transpose(jvp())/reduce_sum | solution.py:33
  344.3 12.0 %fusion.264 = (f32[64,512]{1,0:T(8,128)S(1)}, f32[64,512]{1,0:T(8,128)S(1)}, f32[64,512]{1,0:T(8,128)S(1)}, f32[64,512]{1,0:T(8,128)S(1)}, f32[64,512]{1,0:T(8,1...) fusion(f32[64,512]{1,0:T(8,128)S(1)} %get-tuple-element.803, ...), kind=kLoop, calls=%fused_computation.79.clone.1 | loop fusion | flops 86671360 | bytes 2162944 | tf_op jit(solution)/shard_map/while/body/eval_jaxpr/transpose(jvp())/reduce_sum | solution.py:33
  361.6 12.0 %fusion.264 = (f32[64,512]{1,0:T(8,128)S(1)}, f32[64,512]{1,0:T(8,128)S(1)}, f32[64,512]{1,0:T(8,128)S(1)}, f32[64,512]{1,0:T(8,128)S(1)}, f32[64,512]{1,0:T(8,1...) fusion(f32[64,512]{1,0:T(8,128)S(1)} %get-tuple-element.803, ...), kind=kLoop, calls=%fused_computation.79.clone.1 | loop fusion | flops 86671360 | bytes 2162944 | tf_op jit(solution)/shard_map/while/body/eval_jaxpr/transpose(jvp())/reduce_sum | solution.py:33
  378.8 12.0 %fusion.264 = (f32[64,512]{1,0:T(8,128)S(1)}, f32[64,512]{1,0:T(8,128)S(1)}, f32[64,512]{1,0:T(8,128)S(1)}, f32[64,512]{1,0:T(8,128)S(1)}, f32[64,512]{1,0:T(8,1...) fusion(f32[64,512]{1,0:T(8,128)S(1)} %get-tuple-element.803, ...), kind=kLoop, calls=%fused_computation.79.clone.1 | loop fusion | flops 86671360 | bytes 2162944 | tf_op jit(solution)/shard_map/while/body/eval_jaxpr/transpose(jvp())/reduce_sum | solution.py:33
  396.1 12.0 %fusion.264 = (f32[64,512]{1,0:T(8,128)S(1)}, f32[64,512]{1,0:T(8,128)S(1)}, f32[64,512]{1,0:T(8,128)S(1)}, f32[64,512]{1,0:T(8,128)S(1)}, f32[64,512]{1,0:T(8,1...) fusion(f32[64,512]{1,0:T(8,128)S(1)} %get-tuple-element.803, ...), kind=kLoop, calls=%fused_computation.79.clone.1 | loop fusion | flops 86671360 | bytes 2162944 | tf_op jit(solution)/shard_map/while/body/eval_jaxpr/transpose(jvp())/reduce_sum | solution.py:33
  413.3 12.0 %fusion.264 = (f32[64,512]{1,0:T(8,128)S(1)}, f32[64,512]{1,0:T(8,128)S(1)}, f32[64,512]{1,0:T(8,128)S(1)}, f32[64,512]{1,0:T(8,128)S(1)}, f32[64,512]{1,0:T(8,1...) fusion(f32[64,512]{1,0:T(8,128)S(1)} %get-tuple-element.803, ...), kind=kLoop, calls=%fused_computation.79.clone.1 | loop fusion | flops 86671360 | bytes 2162944 | tf_op jit(solution)/shard_map/while/body/eval_jaxpr/transpose(jvp())/reduce_sum | solution.py:33
  429.0 41.2 %psum.39 = f32[512]{0:T(512)} all-reduce(f32[512]{0:T(512)S(1)} %get-tuple-element.585), channel_id=1, replica_groups=mesh['seq'=16,'batch'=2] {'seq','batch'}, use_global_device_ids=true, to_apply=%region_24.25 | all-reduce | flops 512 | bytes 4096 | tf_op jit(solution)/shard_map/psum | solution.py:156
  470.1 85.4 %all-reduce.3.cloned.1.call-done = (f32[512,64]{0,1:T(8,128)}, f32[512,64]{0,1:T(8,128)}, f32[512,64]{0,1:T(8,128)}, f32[512,64]{0,1:T(8,128)}) async-done(((f32[512,64]{0,1:T(8,128)}, f32[512,64]{0,1:T(8,128)}, f32[512,64]{0,1:T(8,128)}, f32[512,64]{0,1:T(8,128)}), (f32[512,64]{0,1:T(8,128)}, f32[512,64]{0,1:T(8,128)}, f32[512,64]{0,1:T(8,128)}, f32[512,64]{0,1:T(8,128)})) %all-reduce.3.cloned.1.call-update) | async-done | bytes 524304 | tf_op jit(solution)/shard_map/psum | solution.py:156
  (305 shorter events, 134.9 us)
Async XLA Ops:
  7.2 8.9 %copy-start.14 = (bf16[4,128,512]{2,1,0:T(8,128)(2,1)S(1)}, bf16[4,128,512]{2,1,0:T(8,128)(2,1)}, u32[]{:S(2)}) copy-start(bf16[4,128,512]{2,1,0:T(8,128)(2,1)} %param.11) | copy-start | bytes 1572868
  9.5 19.1 %all-to-all-start = ((bf16[4,1,128,512]{3,0,1,2:T(4,128)(2,1)}), bf16[4,1,128,512]{3,0,1,2:T(4,128)(2,1)S(1)}, u32[]{:S(2)}, u32[]{:S(2)}) async-start(bf16[4,1,128,512]{3,0,1,2:T(4,128)(2,1)} %bitcast.253), calls=%async_computation | async-start | bytes 1048576 | tf_op jit(solution)/shard_map/all_to_all | solution.py:109
  28.6 18.3 %all-to-all-start.6 = ((bf16[4,1,128,512]{3,0,1,2:T(4,128)(2,1)}), bf16[4,1,128,512]{3,0,1,2:T(4,128)(2,1)S(1)}, u32[]{:S(2)}, u32[]{:S(2)}) async-start(bf16[4,1,128,512]{3,0,1,2:T(4,128)(2,1)} %bitcast.251), calls=%async_computation.6 | async-start | bytes 1048576 | tf_op jit(solution)/shard_map/all_to_all | solution.py:108
  46.8 1.6 copy-start.6
  51.2 7.2 %copy-start.12 = (bf16[4,8,32,512]{3,2,1,0:T(8,128)(2,1)S(1)}, bf16[4,8,32,512]{3,2,1,0:T(8,128)(2,1)}, u32[]{:S(2)}) copy-start(bf16[4,8,32,512]{3,2,1,0:T(8,128)(2,1)} %get-tuple-element.577) | copy-start | bytes 3145732
  52.7 29.6 %all-to-all-start.7 = ((bf16[4,8,32,512]{3,1,0,2:T(8,128)(2,1)}), bf16[4,8,32,512]{3,1,0,2:T(8,128)(2,1)S(1)}, u32[]{:S(2)}, u32[]{:S(2)}) async-start(bf16[4,8,32,512]{3,1,0,2:T(8,128)(2,1)} %copy.128), calls=%async_computation.7 | async-start | bytes 2097152 | tf_op jit(solution)/shard_map/all_to_all | solution.py:114
  58.4 28.8 %copy-start.17 = (f32[512,64]{0,1:T(8,128)S(1)}, f32[512,64]{0,1:T(8,128)}, u32[]{:S(2)}) copy-start(f32[512,64]{0,1:T(8,128)} %param.13) | copy-start | bytes 393220
  58.4 28.9 %copy-start.15 = (f32[512,64]{0,1:T(8,128)S(1)}, f32[512,64]{0,1:T(8,128)}, u32[]{:S(2)}) copy-start(f32[512,64]{0,1:T(8,128)} %param.14) | copy-start | bytes 393220
  82.3 28.8 %all-to-all-start.8 = ((bf16[4,8,32,512]{3,1,0,2:T(8,128)(2,1)}), bf16[4,8,32,512]{3,1,0,2:T(8,128)(2,1)S(1)}, u32[]{:S(2)}, u32[]{:S(2)}) async-start(bf16[4,8,32,512]{3,1,0,2:T(8,128)(2,1)} %copy.130), calls=%async_computation.8 | async-start | bytes 2097152 | tf_op jit(solution)/shard_map/all_to_all | solution.py:115
  87.8 28.3 %copy-start = (f32[512,64]{0,1:T(8,128)S(1)}, f32[512,64]{0,1:T(8,128)}, u32[]{:S(2)}) copy-start(f32[512,64]{0,1:T(8,128)} %param.15) | copy-start | bytes 393220
  87.8 28.3 %copy-start.1 = (f32[512,64]{0,1:T(8,128)S(1)}, f32[512,64]{0,1:T(8,128)}, u32[]{:S(2)}) copy-start(f32[512,64]{0,1:T(8,128)} %param.16) | copy-start | bytes 393220
  111.1 5.0 copy-start.4
  111.1 61.9 %all-to-all-start.1 = ((bf16[4,8,32,512]{3,1,0,2:T(8,128)(2,1)}), bf16[4,8,32,512]{3,1,0,2:T(8,128)(2,1)}, u32[]{:S(2)}, u32[]{:S(2)}) async-start(bf16[4,8,32,512]{3,1,0,2:T(8,128)(2,1)} %copy.113), calls=%async_computation.1 | async-start | bytes 2097152 | tf_op jit(solution)/shard_map/all_to_all | solution.py:116
  170.0 3.0 copy-start.18
  173.0 7.8 %copy-start.19 = (f32[8,16,2,512]{3,2,1,0:T(2,128)S(1)}, f32[8,16,2,512]{3,2,1,0:T(2,128)}, u32[]{:S(2)}) copy-start(f32[8,16,2,512]{3,2,1,0:T(2,128)} %get-tuple-element.299) | copy-start | bytes 1572868
  173.0 30.4 %all-to-all-start.2 = ((bf16[4,8,32,512]{3,1,0,2:T(8,128)(2,1)}), bf16[4,8,32,512]{3,1,0,2:T(8,128)(2,1)}, u32[]{:S(2)}, u32[]{:S(2)}) async-start(bf16[4,8,32,512]{3,1,0,2:T(8,128)(2,1)} %copy.115), calls=%async_computation.2 | async-start | bytes 2097152 | tf_op jit(solution)/shard_map/all_to_all | solution.py:117
  186.2 2.0 copy-start.5
  203.4 2.7 copy-start.2
  203.4 3.2 copy-start.3
  203.4 3.2 copy-start.7
  216.0 29.0 %all-to-all-start.3 = ((bf16[4,128,2,512]{3,2,0,1:T(2,128)(2,1)}), bf16[4,128,2,512]{3,2,0,1:T(2,128)(2,1)S(1)}, u32[]{:S(2)}, u32[]{:S(2)}) async-start(bf16[4,128,2,512]{3,2,0,1:T(2,128)(2,1)} %copy.118), calls=%async_computation.3 | async-start | bytes 2097152 | tf_op jit(solution)/shard_map/all_to_all | solution.py:131
  223.2 26.8 %copy-start.16 = (f32[512,64]{0,1:T(8,128)S(1)}, f32[512,64]{0,1:T(8,128)}, u32[]{:S(2)}) copy-start(f32[512,64]{0,1:T(8,128)} %param.14) | copy-start | bytes 393220
  223.2 27.3 %copy-start.13 = (f32[128,2,512]{2,0,1:T(8,128)S(1)}, f32[128,2,512]{2,0,1:T(8,128)}, u32[]{:S(2)}) copy-start(f32[128,2,512]{2,0,1:T(8,128)} %get-tuple-element.495) | copy-start | bytes 1572868
  245.0 29.3 %all-to-all-start.4 = ((bf16[4,128,2,512]{3,2,0,1:T(2,128)(2,1)}), bf16[4,128,2,512]{3,2,0,1:T(2,128)(2,1)}, u32[]{:S(2)}, u32[]{:S(2)}) async-start(bf16[4,128,2,512]{3,2,0,1:T(2,128)(2,1)} %copy.120), calls=%async_computation.4 | async-start | bytes 2097152 | tf_op jit(solution)/shard_map/all_to_all | solution.py:132
  282.4 144.1 %all-to-all-start.5 = ((bf16[4,16,8,512]{3,2,0,1:T(8,128)(2,1)}), bf16[4,16,8,512]{3,2,0,1:T(8,128)(2,1)}, u32[]{:S(2)}, u32[]{:S(2)}) async-start(bf16[4,16,8,512]{3,2,0,1:T(8,128)(2,1)} %copy.122), calls=%async_computation.5 | async-start | bytes 1048576 | tf_op jit(solution)/shard_map/all_to_all | solution.py:134
  287.7 267.8 %all-reduce.3.cloned.1.call-start = ((), (), s32[]{:S(2)}) async-start(), calls=%async_computation.9 | async-start | bytes 1048576 | tf_op jit(solution)/shard_map/psum | solution.py:156
  287.7 138.8 %copy-start.20 = (f32[512]{0:T(512)S(1)}, f32[512]{0:T(512)}, u32[]{:S(2)}) copy-start(f32[512]{0:T(512)} %param.17) | copy-start | bytes 6148
  425.7 0.7 copy-start.8
  425.7 0.7 copy-start.9
  425.7 0.7 copy-start.10
  425.8 0.7 copy-start.11
Sparse Core Ops, SparseCore 0:
  426.6 128.8 all-reduce.2
where the time goes:
time: 575 us; the launch traced here: 569 us
  waiting for transfers between devices  198 us (34%)
  other arithmetic  161 us (28%)
  local copies, waits for them, and re-layouts  58.4 us (10%)
  starting transfers between devices  49.8 us (9%)
  blocking collectives  41.2 us (7%)
  matrix products  29.2 us (5%)
  loops' own time  16.8 us (3%)
  between operations  14.4 us (3%)
    reduce_sum x8, other arithmetic, spectrum_terms(): diff_upper = z_imag - pole_imag  96.2 us
    psum x1, waiting for transfers between devices, local(): lax.psum((pulled[0], pulled[1], pulled[2], pulled[3], passthrough_part),...  85.4 us
    psum x1, blocking collectives, local(): lax.psum((pulled[0], pulled[1], pulled[2], pulled[3], passthrough_part),...  41.2 us
    reduce_sum x8, other arithmetic, spectrum_terms(): return (jnp.sum(part_real, axis=1), jnp.sum(part_imag, axis=1))  34.8 us
    dot_general x18, matrix products, matmul(): return jnp.einsum(form, left, right, preferred_element_type=jnp.float32)  29.2 us
    all_to_all x1, waiting for transfers between devices, local(): lax.all_to_all(in_g_real, 'seq', split_axis=2, concat_axis=1, tiled=True)  22.3 us
    all_to_all x1, waiting for transfers between devices, local(): lax.all_to_all(turned_real, 'seq', split_axis=1, concat_axis=2, tiled=True)  21.8 us
    all_to_all x1, waiting for transfers between devices, local(): lax.all_to_all(in_g_imag, 'seq', split_axis=2, concat_axis=1, tiled=True)  20.4 us
  transfers between devices with their start and end apart: 10, of which 8 were waited for; matrix products, arithmetic and copies ran while one was open for 37% of the time, Pallas kernels for 0%

commit v1 on v0

v1 whole, which is shorter than its diff:
```python
import math

import jax
import jax.numpy as jnp
from jax import lax
from jax.sharding import PartitionSpec as P

TWO_PI = 2.0 * math.pi
AXES = ("seq", "batch")
HIGH = lax.Precision.HIGH


def cos_sin(numerator, length):
    phases = (numerator % length).astype(jnp.float32) * (TWO_PI / length)
    return (jnp.cos(phases), jnp.sin(phases))


def cmul(a, b):
    return (a[0] * b[0] - a[1] * b[1], a[0] * b[1] + a[1] * b[0])


def cdiv(a, b):
    inv = 1.0 / (b[0] * b[0] + b[1] * b[1])
    return ((a[0] * b[0] + a[1] * b[1]) * inv, (a[1] * b[0] - a[0] * b[1]) * inv)


def powers(rate, angle, step, count):
    turn = angle * step
    laps = jnp.round(turn * (1.0 / TWO_PI))
    turn = (turn - laps * 6.28125) - laps * (TWO_PI - 6.28125)
    n = jnp.arange(count, dtype=jnp.float32)
    size = jnp.exp(-(rate * step)[..., None] * n)
    phase = turn[..., None] * n
    return (size * jnp.cos(phase), size * jnp.sin(phase))


def local(inputs, out_grad, log_rate, pole_angle, weight_real, weight_imag, passthrough):
    batch_rows, slice_len, channels = inputs.shape
    rows = lax.axis_size("seq")
    copies = lax.axis_size("batch")
    devices = rows * copies
    own_ch = channels // devices
    batch = batch_rows * copies
    freq_rows = 2 * rows
    half = rows + 1
    n_freq = freq_rows * slice_len
    me = lax.axis_index("seq") * copies + lax.axis_index("batch")

    def to_channels(x):
        x = x.reshape(batch_rows, slice_len, devices, own_ch).transpose(2, 0, 3, 1)
        x = lax.all_to_all(x, AXES, split_axis=0, concat_axis=0, tiled=True)
        return x.reshape(rows, batch, own_ch, slice_len)

    grad_cols = to_channels(out_grad)
    in_cols = to_channels(inputs)

    k_index = jnp.arange(half, dtype=jnp.int32)
    r_index = jnp.arange(freq_rows, dtype=jnp.int32)
    m_index = jnp.arange(slice_len, dtype=jnp.int32)
    cos_one, sin_one = cos_sin(k_index[:, None] * r_index[None, :], freq_rows)
    table_one = jnp.stack([cos_one, -sin_one], axis=1)
    cos_two, sin_two = cos_sin(m_index[:, None] * m_index[None, :], slice_len)
    turn_real, turn_imag = cos_sin(k_index[:, None] * m_index[None, :], n_freq)
    full_cos = turn_real[:, :, None] * cos_two - turn_imag[:, :, None] * sin_two
    full_sin = turn_imag[:, :, None] * cos_two + turn_real[:, :, None] * sin_two
    table_two = jnp.concatenate(
        [
            jnp.concatenate([full_cos, -full_sin], axis=2),
            jnp.concatenate([full_sin, full_cos], axis=2),
        ],
        axis=1,
    )
    ends = (k_index == 0) | (k_index == rows)
    share = jnp.where(ends, 1.0, 2.0).astype(jnp.float32)[:, None, None] / n_freq
    table_back = table_one * share
    one16 = table_one.astype(jnp.bfloat16)
    two16 = table_two.astype(jnp.bfloat16)
    back16 = (table_one * (share * n_freq)).astype(jnp.bfloat16)

    def own(p):
        return lax.dynamic_slice_in_dim(p, me * own_ch, own_ch, 0)

    rate = jnp.exp(own(log_rate))
    angle = own(pole_angle)
    w_real, w_imag = own(weight_real), own(weight_imag)
    shrink = jnp.sqrt(-jnp.expm1(-2.0 * rate))
    weight = (w_real * shrink, w_imag * shrink)
    fine = powers(rate, angle, 1.0, slice_len)
    coarse = powers(rate, angle, float(slice_len), freq_rows + 1)
    whole = (coarse[0][..., -1], coarse[1][..., -1])
    coarse = (coarse[0][..., :-1], coarse[1][..., :-1])
    lam = (fine[0][..., 1], fine[1][..., 1])
    gap = (1.0 - whole[0], -whole[1])
    bottom = cmul(lam, gap)
    lead = cdiv(weight, bottom)
    tail = 2.0 * jnp.sum(cdiv(weight, lam)[0], axis=1)
    lead_rows = cmul((lead[0][..., None], lead[1][..., None]), coarse)
    taps = jnp.einsum(
        "xsr,xsm->rxm",
        jnp.concatenate([2.0 * lead_rows[0], -2.0 * lead_rows[1]], axis=1),
        jnp.concatenate(fine, axis=1),
        precision=HIGH,
    )
    kern = jnp.einsum("kir,rxm->kxim", table_one, taps, precision=HIGH)
    kern = jnp.einsum("kxa,kab->kxb", kern.reshape(half, own_ch, -1), table_two, precision=HIGH)
    kern_real = kern[:, :, :slice_len] - tail[None, :, None]
    kern_imag = kern[:, :, slice_len:]

    def forward(x):
        g = jnp.einsum("kir,rbxm->kbxim", one16[:, :, :rows], x, preferred_element_type=jnp.float32)
        g = g.astype(jnp.bfloat16).reshape(half, batch, own_ch, 2 * slice_len)
        s = jnp.einsum("kbxa,kac->kbxc", g, two16, preferred_element_type=jnp.float32)
        return s[..., :slice_len], s[..., slice_len:]

    out_real, out_imag = forward(grad_cols)
    kr, ki = kern_real[:, None], kern_imag[:, None]
    prod = jnp.concatenate(
        [(kr * out_real + ki * out_imag) / n_freq, (kr * out_imag - ki * out_real) / n_freq],
        axis=3,
    ).astype(jnp.bfloat16)
    back = jnp.einsum("kbxc,kac->kbxa", prod, two16, preferred_element_type=jnp.float32)
    back = back.astype(jnp.bfloat16).reshape(half, batch, own_ch, 2, slice_len)
    conv = jnp.einsum("kir,kbxim->rbxm", back16[:, :, :rows], back, preferred_element_type=jnp.float32)
    conv = conv.astype(jnp.bfloat16).reshape(devices, batch_rows, own_ch, slice_len)
    conv = lax.all_to_all(conv, AXES, split_axis=0, concat_axis=0, tiled=True)
    conv = conv.transpose(1, 3, 0, 2).reshape(batch_rows, slice_len, channels)
    input_grad = (conv.astype(jnp.float32) + passthrough * out_grad.astype(jnp.float32)).astype(
        jnp.bfloat16
    )

    in_real, in_imag = forward(in_cols)
    cross = jnp.concatenate(
        [
            jnp.sum(out_real * in_real + out_imag * in_imag, axis=1),
            jnp.sum(out_imag * in_real - out_real * in_imag, axis=1),
        ],
        axis=2,
    )
    corr = jnp.einsum("kxc,kac->kxa", cross, table_two, precision=HIGH)
    corr = jnp.einsum(
        "kir,kxim->xrm", table_back, corr.reshape(half, own_ch, 2, slice_len), precision=HIGH
    )
    steps = jnp.arange(slice_len, dtype=jnp.float32)
    sums = jnp.einsum(
        "xsm,xrm->xsr",
        jnp.concatenate([fine[0], fine[1], steps * fine[0], steps * fine[1]], axis=1),
        corr,
        precision=HIGH,
    )
    states = rate.shape[1]
    low = (sums[:, :states], sums[:, states : 2 * states])
    low_step = (sums[:, 2 * states : 3 * states], sums[:, 3 * states :])
    far = jnp.arange(freq_rows, dtype=jnp.float32) * slice_len
    t0 = tuple(jnp.sum(v, axis=2) for v in cmul(coarse, low))
    t1 = tuple(
        jnp.sum(v, axis=2)
        for v in cmul(coarse, (low[0] * far + low_step[0], low[1] * far + low_step[1]))
    )
    corr0 = corr[:, 0, 0][:, None]
    near = cdiv((corr0, jnp.zeros_like(corr0)), lam)
    top = cdiv(t0, bottom)
    h = (top[0] - near[0], top[1] - near[1])
    d = cdiv(t1, bottom)
    ratio = cdiv((1.0 - (n_freq + 1.0) * whole[0], -(n_freq + 1.0) * whole[1]), gap)
    lower = cmul(top, ratio)
    d = (d[0] - lower[0] + near[0], d[1] - lower[1] + near[1])
    wd = cmul(weight, d)
    wr_grad = 2.0 * shrink * h[0]
    wi_grad = -2.0 * shrink * h[1]
    angle_grad = -2.0 * wd[1]
    shrink_part = 2.0 * (w_real * h[0] - w_imag * h[1]) * jnp.exp(-2.0 * rate) / shrink
    rate_grad = rate * (shrink_part - 2.0 * wd[0])
    pass_part = jnp.sum(
        in_cols.astype(jnp.float32) * grad_cols.astype(jnp.float32), axis=(0, 1, 3)
    )
    packed = jnp.concatenate([rate_grad, angle_grad, wr_grad, wi_grad, jnp.broadcast_to(pass_part[:, None], rate.shape)], axis=1)
    packed = lax.all_gather(packed, AXES, axis=0, tiled=True)
    return (
        input_grad,
        packed[:, :states],
        packed[:, states : 2 * states],
        packed[:, 2 * states : 3 * states],
        packed[:, 3 * states : 4 * states],
        packed[:, 4 * states],
    )


def solution(mesh):
    placed = (P("batch", "seq", None), P("batch", "seq", None), P(), P(), P(), P(), P())
    return jax.shard_map(
        local,
        mesh=mesh,
        in_specs=placed,
        out_specs=(P("batch", "seq", None), P(), P(), P(), P(), P()),
        check_vma=False,
    )
```

time: 575 us -> 132 us (0.23)
  the two profiles are of different devices: /device:TPU:15 before, /device:TPU:0 now
where the time goes in v1:
time: 132 us; the launch traced here: 131 us
  blocking collectives  45.6 us (35%)
  local copies, waits for them, and re-layouts  27.4 us (21%)
  matrix products  17.5 us (13%)
  starting transfers between devices  13.5 us (10%)
  waiting for transfers between devices  13 us (10%)
  other arithmetic  12.9 us (10%)
    all_gather x1, blocking collectives, local(): packed = lax.all_gather(packed, AXES, axis=0, tiled=True)  45.6 us
    all_to_all x2, waiting for transfers between devices, to_channels(): x = lax.all_to_all(x, AXES, split_axis=0, concat_axis=0, tiled=True)  13 us
    unnamed x83, local copies, waits for them, and re-layouts  10.8 us
    all_to_all x2, starting transfers between devices, to_channels(): x = lax.all_to_all(x, AXES, split_axis=0, concat_axis=0, tiled=True)  10.4 us
    dot_general x2, matrix products, forward(): jnp.einsum('kbxa,kac->kbxc', g, two16, preferred_element_type=jnp.float32)  3.67 us
    dot_general x1, matrix products, local(): jnp.einsum('kxa,kab->kxb', kern.reshape(half, own_ch, -1), table_two, pre...  3.57 us
    mul x1, other arithmetic, local(): steps * fine[0]  3.15 us
    reshape x2, local copies, waits for them, and re-layouts, forward(): g = g.astype(jnp.bfloat16).reshape(half, batch, own_ch, 2 * slice_len)  3.14 us
  transfers between devices with their start and end apart: 3, of which 2 were waited for; matrix products, arithmetic and copies ran while one was open for 17% of the time, Pallas kernels for 0%

profile of v1, /device:TPU:0, one launch (start us, length us, event | category | flops | bytes accessed | tf_op | source)
XLA Modules:
  0.0 131.1 jit_solution(11048607904030733533)
XLA Ops:
  0.6 1.3 copy.133
  2.0 0.9 copy.134
  2.8 7.3 %all-to-all-start = ((bf16[32,4,16,128]{3,2,1,0:T(8,128)(2,1)}), bf16[32,4,16,128]{3,2,1,0:T(8,128)(2,1)S(1)}, u32[]{:S(2)}, u32[]{:S(2)}) async-start(bf16[32,4,16,128]{3,2,1,0:T(8,128)(2,1)} %copy.134), calls=%async_computation | async-start | bytes 1048576 | tf_op jit(solution)/shard_map/all_to_all | solution.py:51
  10.3 0.9 constant_dynamic-slice_fusion.2
  11.2 0.9 constant_dynamic-slice_fusion
  12.8 0.9 copy.144
  14.1 3.1 %iota_multiply_fusion.1 = (f32[16,64,128]{2,1,0:T(8,128)}, f32[16,64,128]{2,1,0:T(8,128)}, f32[16,64,128]{2,1,0:T(8,128)S(1)}, f32[16,64,128]{2,1,0:T(8,128)S(1)}) fusion(f32[16,64]{1,0:T(8,128)S(1)} %get-tuple-element.83, f32[16,64]{1,0:T(8,128)S(1)} %get-tuple-element.81), kind=kLoop, calls=%fused_computation.52 | loop fusion | flops 786432 | bytes 2105344 | tf_op jit(solution)/shard_map/mul | solution.py:146
  17.3 1.0 slice_reduce_fusion
  18.3 7.4 %all-to-all-done = bf16[32,4,16,128]{3,2,1,0:T(8,128)(2,1)S(1)} async-done(((bf16[32,4,16,128]{3,2,1,0:T(8,128)(2,1)}), bf16[32,4,16,128]{3,2,1,0:T(8,128)(2,1)S(1)}, u32[]{:S(2)}, u32[]{:S(2)}) %all-to-all-start) | async-done | bytes 524320 | tf_op jit(solution)/shard_map/all_to_all | solution.py:51
  25.7 3.1 %all-to-all-start.2 = ((bf16[32,4,16,128]{3,2,1,0:T(8,128)(2,1)}), bf16[32,4,16,128]{3,2,1,0:T(8,128)(2,1)S(1)}, u32[]{:S(2)}, u32[]{:S(2)}) async-start(bf16[32,4,16,128]{3,2,1,0:T(8,128)(2,1)} %copy.144), calls=%async_computation.2 | async-start | bytes 1048576 | tf_op jit(solution)/shard_map/all_to_all | solution.py:51
  30.6 1.0 slice_reduce_fusion.1
  31.6 1.7 %cosine_multiply_fusion.1 = (f32[16,64,33]{1,0,2:T(8,128)S(1)}, f32[16,64,33]{1,0,2:T(8,128)}) fusion(f32[16,64]{1,0:T(8,128)S(1)} %get-tuple-element.82, f32[16,64]{1,0:T(8,128)S(1)} %get-tuple-element.80), kind=kLoop, calls=%fused_computation.63 | loop fusion | flops 135168 | bytes 278528 | tf_op jit(solution)/shard_map/mul | solution.py:34
  33.3 2.1 %fusion.48 = (f32[17,128,128]{2,1,0:T(8,128)}, f32[17,128,128]{2,1,0:T(8,128)}, f32[17,128,128]{2,1,0:T(8,128)}) fusion(f32[128,128]{1,0:T(8,128)S(1)} %get-tuple-element.86, f32[17,128]{1,0:T(8,128)S(1)} %get-tuple-element.89, f32[128,128]{1,0:T(8,128)S(1)} %get-tuple-element.87, f32[17,128]{1,0:T(8,128)S(1)} %get-tuple-element.88), kind=kLoop, calls=%fused_computation.78 | loop fusion | flops 1949696 | bytes 3490816 | tf_op jit(solution)/shard_map/neg | solution.py:68
  36.0 1.2 copy.137
  37.2 1.6 %reshape.232 = bf16[17,8,16,256]{3,2,1,0:T(8,128)(2,1)} reshape(bf16[17,8,16,2,128]{4,3,2,1,0:T(2,128)(2,1)S(1)} %copy.137) | data formatting | bytes 2228224 | tf_op jit(solution)/shard_map/reshape | solution.py:111
  38.7 5.6 %all-to-all-done.2 = bf16[32,4,16,128]{3,2,1,0:T(8,128)(2,1)S(1)} async-done(((bf16[32,4,16,128]{3,2,1,0:T(8,128)(2,1)}), bf16[32,4,16,128]{3,2,1,0:T(8,128)(2,1)S(1)}, u32[]{:S(2)}, u32[]{:S(2)}) %all-to-all-start.2) | async-done | bytes 524320 | tf_op jit(solution)/shard_map/all_to_all | solution.py:51
  44.9 1.2 copy.147
  46.1 1.6 %reshape.237 = bf16[17,8,16,256]{3,2,1,0:T(8,128)(2,1)} reshape(bf16[17,8,16,2,128]{4,3,2,1,0:T(2,128)(2,1)S(1)} %copy.147) | data formatting | bytes 2228224 | tf_op jit(solution)/shard_map/reshape | solution.py:111
  47.7 3.2 %fusion.4 = f32[17,8,16,256]{3,2,1,0:T(8,128)S(1)} fusion(bf16[17,8,16,256]{3,2,1,0:T(8,128)(2,1)} %reshape.232, f32[17,128,128]{2,1,0:T(8,128)} %get-tuple-element.67, f32[17,128,128]{2,1,0:T(8,128)} %get-tuple-element.66, f32[17,128,128]{2,1,0:T(8,128)} %get-tuple-element.65), kind=kOutput, calls=%fused_computation.5 | convolution fusion | flops 294125568 | bytes 6684672 | tf_op jit(solution)/shard_map/kbxa,kac->kbxc/dot_general | solution.py:112
  52.4 2.7 %fusion.14 = f32[17,16,256]{2,1,0:T(8,128)} fusion(f32[17,128,128]{2,1,0:T(8,128)S(1)} %copy-done.12, f32[17,128,128]{2,1,0:T(8,128)S(1)} %copy-done.10, f32[17,128,128]{2,1,0:T(8,128)S(1)} %copy-done.8, f32[17,16,128]{2,1,0:T(8,128)S(1)} %get-tuple-element.37, f32[17,16,128]{2,1,0:T(8,128)S(1)} %get-tuple-element.36), kind=kOutput, calls=%fused_computation.15 | convolution fusion | flops 110366720 | bytes 3899392 | tf_op jit(solution)/shard_map/kxc,kac->kxa/dot_general | solution.py:139
  55.1 1.8 %reshape.238 = f32[17,16,2,128]{3,2,1,0:T(2,128)} reshape(f32[17,16,256]{2,1,0:T(8,128)} %fusion.14) | data formatting | bytes 557056 | tf_op jit(solution)/shard_map/reshape | solution.py:141
  56.9 1.4 %fusion.41 = f32[16,128,32,1]{1,2,3,0:T(8,128)S(1)} fusion(f32[17,16,2,128]{3,2,1,0:T(2,128)} %reshape.238, f32[17,1,32]{2,0,1:T(8,128)} %copy-done.15, f32[17,1,32]{2,0,1:T(8,128)} %copy-done.17, f32[17]{0:T(128)} %get-tuple-element.91), kind=kOutput, calls=%fused_computation.57 | convolution fusion | flops 13371520 | bytes 545092 | tf_op jit(solution)/shard_map/kir,kxim->xrm/dot_general | solution.py:140
  58.3 2.5 %fusion.6 = f32[16,256,32]{1,2,0:T(8,128)S(1)} fusion(f32[16,64,128]{2,1,0:T(8,128)} %get-tuple-element.75, f32[16,64,128]{2,1,0:T(8,128)} %get-tuple-element.74, f32[16,64,128]{2,1,0:T(8,128)S(1)} %get-tuple-element.76, f32[16,64,128]{2,1,0:T(8,128)} %copy-done, f32[16,128,32,1]{1,2,3,0:T(8,128)S(1)} %fusion.41), kind=kOutput, calls=%fused_computation.7 | convolution fusion | flops 102236160 | bytes 2883584 | tf_op jit(solution)/shard_map/xsm,xrm->xsr/dot_general | solution.py:144
  63.2 1.4 %multiply_multiply_fusion.1 = (f32[16,64]{1,0:T(8,128)}, f32[16,64]{1,0:T(8,128)}, f32[16,64]{1,0:T(8,128)}, f32[16,64]{1,0:T(8,128)}, f32[16,64]{1,0:T(8,128)},...) fusion(f32[16,64]{1,0:T(8,128)S(1)} %copy.170, f32[16,64]{1,0:T(8,128)S(1)} %copy-done.19, ...), kind=kLoop, calls=%fused_computation.142 | loop fusion | flops 84976 | bytes 82048 | tf_op jit(solution)/shard_map/mul | solution.py:168
  65.8 0.9 reshape.229
  66.8 3.6 %fusion.16 = f32[17,16,256]{2,1,0:T(8,128)S(1)} fusion(f32[17,16,256]{2,1,0:T(8,128)} %reshape.229, f32[17,128,128]{2,1,0:T(8,128)} %get-tuple-element.67, f32[17,128,128]{2,1,0:T(8,128)} %get-tuple-element.66, f32[17,128,128]{2,1,0:T(8,128)} %get-tuple-element.65), kind=kOutput, calls=%fused_computation.17 | convolution fusion | flops 110297088 | bytes 3899392 | tf_op jit(solution)/shard_map/kxa,kab->kxb/dot_general | solution.py:105
  70.9 0.8 copy-done.9
  72.4 0.9 fusion.19
  74.7 0.9 copy.140
  75.7 3.1 %all-to-all-start.1 = ((bf16[32,4,16,128]{3,2,1,0:T(8,128)(2,1)}), bf16[32,4,16,128]{3,2,1,0:T(8,128)(2,1)S(1)}, u32[]{:S(2)}, u32[]{:S(2)}) async-start(bf16[32,4,16,128]{3,2,1,0:T(8,128)(2,1)} %bitcast.18), calls=%async_computation.1 | async-start | bytes 1048576 | tf_op jit(solution)/shard_map/all_to_all | solution.py:125
  79.4 45.6 %all_gather.3 = f32[512,320]{1,0:T(8,128)S(1)} all-gather(f32[16,320]{1,0:T(8,128)S(1)} %concatenate.36), channel_id=1, replica_groups=mesh['seq'=16,'batch'=2] {'seq','batch'}, dimensions={0}, use_global_device_ids=true | all-gather | bytes 675840 | tf_op jit(solution)/shard_map/all_gather | solution.py:177
  130.1 1.0 copy.153
  (115 shorter events, 17.6 us)
Async XLA Ops:
  1.9 10.6 %copy-start.14 = (bf16[4,128,512]{2,1,0:T(8,128)(2,1)S(1)}, bf16[4,128,512]{2,1,0:T(8,128)(2,1)}, u32[]{:S(2)}) copy-start(bf16[4,128,512]{2,1,0:T(8,128)(2,1)} %param.7) | copy-start | bytes 1572868
  2.8 22.9 %all-to-all-start = ((bf16[32,4,16,128]{3,2,1,0:T(8,128)(2,1)}), bf16[32,4,16,128]{3,2,1,0:T(8,128)(2,1)S(1)}, u32[]{:S(2)}, u32[]{:S(2)}) async-start(bf16[32,4,16,128]{3,2,1,0:T(8,128)(2,1)} %copy.134), calls=%async_computation | async-start | bytes 1048576 | tf_op jit(solution)/shard_map/all_to_all | solution.py:51
  10.2 34.1 %copy-start.15 = (f32[17,1,32]{2,0,1:T(8,128)}, f32[17,1,32]{2,0,1:T(8,128)S(1)}, u32[]{:S(2)}) copy-start(f32[17,1,32]{2,0,1:T(8,128)S(1)} %get-tuple-element.84) | copy-start | bytes 6532
  10.2 34.1 %copy-start.17 = (f32[17,1,32]{2,0,1:T(8,128)}, f32[17,1,32]{2,0,1:T(8,128)S(1)}, u32[]{:S(2)}) copy-start(f32[17,1,32]{2,0,1:T(8,128)S(1)} %get-tuple-element.85) | copy-start | bytes 6532
  17.3 16.0 %copy-start = (f32[16,64,128]{2,1,0:T(8,128)}, f32[16,64,128]{2,1,0:T(8,128)S(1)}, u32[]{:S(2)}) copy-start(f32[16,64,128]{2,1,0:T(8,128)S(1)} %get-tuple-element.77) | copy-start | bytes 1572868
  25.7 9.7 %copy-start.2 = (bf16[32,4,16,128]{3,2,1,0:T(8,128)(2,1)}, bf16[32,4,16,128]{3,2,1,0:T(8,128)(2,1)S(1)}, u32[]{:S(2)}) copy-start(bf16[32,4,16,128]{3,2,1,0:T(8,128)(2,1)S(1)} %all-to-all-done) | copy-start | bytes 1572868
  25.7 18.6 %all-to-all-start.2 = ((bf16[32,4,16,128]{3,2,1,0:T(8,128)(2,1)}), bf16[32,4,16,128]{3,2,1,0:T(8,128)(2,1)S(1)}, u32[]{:S(2)}, u32[]{:S(2)}) async-start(bf16[32,4,16,128]{3,2,1,0:T(8,128)(2,1)} %copy.144), calls=%async_computation.2 | async-start | bytes 1048576 | tf_op jit(solution)/shard_map/all_to_all | solution.py:51
  44.3 1.8 %copy-start.4 = (bf16[32,4,16,128]{3,2,1,0:T(8,128)(2,1)}, bf16[32,4,16,128]{3,2,1,0:T(8,128)(2,1)S(1)}, u32[]{:S(2)}) copy-start(bf16[32,4,16,128]{3,2,1,0:T(8,128)(2,1)S(1)} %all-to-all-done.2) | copy-start | bytes 1572868
  47.7 3.2 %copy-start.7 = (bf16[17,8,16,256]{3,2,1,0:T(8,128)(2,1)S(1)}, bf16[17,8,16,256]{3,2,1,0:T(8,128)(2,1)}, u32[]{:S(2)}) copy-start(bf16[17,8,16,256]{3,2,1,0:T(8,128)(2,1)} %reshape.237) | copy-start | bytes 3342340
  47.7 3.2 %copy-start.8 = (f32[17,128,128]{2,1,0:T(8,128)S(1)}, f32[17,128,128]{2,1,0:T(8,128)}, u32[]{:S(2)}) copy-start(f32[17,128,128]{2,1,0:T(8,128)} %get-tuple-element.65) | copy-start | bytes 3342340
  47.7 3.6 %copy-start.10 = (f32[17,128,128]{2,1,0:T(8,128)S(1)}, f32[17,128,128]{2,1,0:T(8,128)}, u32[]{:S(2)}) copy-start(f32[17,128,128]{2,1,0:T(8,128)} %get-tuple-element.66) | copy-start | bytes 3342340
  47.7 3.9 %copy-start.12 = (f32[17,128,128]{2,1,0:T(8,128)S(1)}, f32[17,128,128]{2,1,0:T(8,128)}, u32[]{:S(2)}) copy-start(f32[17,128,128]{2,1,0:T(8,128)} %get-tuple-element.67) | copy-start | bytes 3342340
  61.0 1.5 %copy-start.19 = (f32[16,64]{1,0:T(8,128)S(1)}, f32[16,64]{1,0:T(8,128)}, u32[]{:S(2)}) copy-start(f32[16,64]{1,0:T(8,128)} %slice_reduce_fusion) | copy-start | bytes 12292
  61.0 1.5 %copy-start.20 = (f32[16,64]{1,0:T(8,128)S(1)}, f32[16,64]{1,0:T(8,128)}, u32[]{:S(2)}) copy-start(f32[16,64]{1,0:T(8,128)} %slice_reduce_fusion.1) | copy-start | bytes 12292
  61.1 2.1 %copy-start.21 = (f32[16,64]{1,0:T(8,128)S(1)}, f32[16,64]{1,0:T(8,128)}, u32[]{:S(2)}) copy-start(f32[16,64]{1,0:T(8,128)} %copy.172) | copy-start | bytes 12292
  61.1 2.1 %copy-start.23 = (f32[16,64]{1,0:T(8,128)S(1)}, f32[16,64]{1,0:T(8,128)}, u32[]{:S(2)}) copy-start(f32[16,64]{1,0:T(8,128)} %copy.173) | copy-start | bytes 12292
  62.5 2.3 %copy-start.1 = (f32[16,64,128]{2,1,0:T(8,128)S(1)}, f32[16,64,128]{2,1,0:T(8,128)}, u32[]{:S(2)}) copy-start(f32[16,64,128]{2,1,0:T(8,128)} %copy-done) | copy-start | bytes 1572868
  66.8 3.6 %copy-start.35 = (f32[16]{0:T(128)S(1)}, f32[16]{0:T(128)}, u32[]{:S(2)}) copy-start(f32[16]{0:T(128)} %get-tuple-element.71) | copy-start | bytes 196
  70.4 1.6 %copy-start.11 = (f32[17,128,128]{2,1,0:T(8,128)S(1)}, f32[17,128,128]{2,1,0:T(8,128)}, u32[]{:S(2)}) copy-start(f32[17,128,128]{2,1,0:T(8,128)} %get-tuple-element.66) | copy-start | bytes 3342340
  70.5 1.9 %copy-start.13 = (f32[17,128,128]{2,1,0:T(8,128)S(1)}, f32[17,128,128]{2,1,0:T(8,128)}, u32[]{:S(2)}) copy-start(f32[17,128,128]{2,1,0:T(8,128)} %get-tuple-element.67) | copy-start | bytes 3342340
  74.7 4.1 %copy-start.3 = (bf16[32,4,16,128]{3,2,1,0:T(8,128)(2,1)S(1)}, bf16[32,4,16,128]{3,2,1,0:T(8,128)(2,1)}, u32[]{:S(2)}) copy-start(bf16[32,4,16,128]{3,2,1,0:T(8,128)(2,1)} %copy-done.2) | copy-start | bytes 1572868
  74.7 4.1 %copy-start.5 = (bf16[32,4,16,128]{3,2,1,0:T(8,128)(2,1)S(1)}, bf16[32,4,16,128]{3,2,1,0:T(8,128)(2,1)}, u32[]{:S(2)}) copy-start(bf16[32,4,16,128]{3,2,1,0:T(8,128)(2,1)} %copy-done.4) | copy-start | bytes 1572868
  75.6 3.5 %copy-start.22 = (f32[16,64]{1,0:T(8,128)S(1)}, f32[16,64]{1,0:T(8,128)}, u32[]{:S(2)}) copy-start(f32[16,64]{1,0:T(8,128)} %copy.172) | copy-start | bytes 12292
  75.6 3.5 %copy-start.24 = (f32[16,64]{1,0:T(8,128)S(1)}, f32[16,64]{1,0:T(8,128)}, u32[]{:S(2)}) copy-start(f32[16,64]{1,0:T(8,128)} %copy.173) | copy-start | bytes 12292
  75.6 3.5 %copy-start.27 = (f32[16,64]{1,0:T(8,128)S(1)}, f32[16,64]{1,0:T(8,128)}, u32[]{:S(2)}) copy-start(f32[16,64]{1,0:T(8,128)} %get-tuple-element.47) | copy-start | bytes 12292
  75.6 3.5 %copy-start.28 = (f32[16,64]{1,0:T(8,128)S(1)}, f32[16,64]{1,0:T(8,128)}, u32[]{:S(2)}) copy-start(f32[16,64]{1,0:T(8,128)} %get-tuple-element.69) | copy-start | bytes 12292
  75.6 3.5 %copy-start.29 = (f32[16,64]{1,0:T(8,128)S(1)}, f32[16,64]{1,0:T(8,128)}, u32[]{:S(2)}) copy-start(f32[16,64]{1,0:T(8,128)} %get-tuple-element.70) | copy-start | bytes 12292
  75.7 3.5 %copy-start.31 = (f32[16,64]{1,0:T(8,128)S(1)}, f32[16,64]{1,0:T(8,128)}, u32[]{:S(2)}) copy-start(f32[16,64]{1,0:T(8,128)} %get-tuple-element.43) | copy-start | bytes 12292
  75.7 3.7 %copy-start.25 = (f32[16,64]{1,0:T(8,128)S(1)}, f32[16,64]{1,0:T(8,128)}, u32[]{:S(2)}) copy-start(f32[16,64]{1,0:T(8,128)} %get-tuple-element.46) | copy-start | bytes 12292
  75.7 3.6 %copy-start.26 = (f32[16,64]{1,0:T(8,128)S(1)}, f32[16,64]{1,0:T(8,128)}, u32[]{:S(2)}) copy-start(f32[16,64]{1,0:T(8,128)} %get-tuple-element.68) | copy-start | bytes 12292
  75.7 3.6 %copy-start.30 = (f32[16,64]{1,0:T(8,128)S(1)}, f32[16,64]{1,0:T(8,128)}, u32[]{:S(2)}) copy-start(f32[16,64]{1,0:T(8,128)} %get-tuple-element.42) | copy-start | bytes 12292
  75.7 53.4 %all-to-all-start.1 = ((bf16[32,4,16,128]{3,2,1,0:T(8,128)(2,1)}), bf16[32,4,16,128]{3,2,1,0:T(8,128)(2,1)S(1)}, u32[]{:S(2)}, u32[]{:S(2)}) async-start(bf16[32,4,16,128]{3,2,1,0:T(8,128)(2,1)} %bitcast.18), calls=%async_computation.1 | async-start | bytes 1048576 | tf_op jit(solution)/shard_map/all_to_all | solution.py:125
  (7 other events, 5.9 us)

commit v2 on v1

--- a/solution.py
+++ b/solution.py
@@ -3,6 +3,8 @@
 import jax
 import jax.numpy as jnp
 from jax import lax
+from jax.experimental import pallas as pl
+from jax.experimental.pallas import tpu as pltpu
 from jax.sharding import PartitionSpec as P
 
 TWO_PI = 2.0 * math.pi
@@ -32,6 +34,75 @@
     size = jnp.exp(-(rate * step)[..., None] * n)
     phase = turn[..., None] * n
     return (size * jnp.cos(phase), size * jnp.sin(phase))
+
+
+def peer_of(place, copies):
+    return {"seq": place // copies, "batch": place % copies}
+
+
+def exchange_kernel(devices, copies, conv, grads, conv_out, grads_out, sems):
+    me = lax.axis_index("seq") * copies + lax.axis_index("batch")
+    barrier = pltpu.get_barrier_semaphore()
+
+    def greet(d, carry):
+        pl.semaphore_signal(
+            barrier,
+            inc=1,
+            device_id=peer_of((me + d) % devices, copies),
+            device_id_type=pl.DeviceIdType.MESH,
+        )
+        return carry
+
+    lax.fori_loop(1, devices, greet, 0)
+    pl.semaphore_wait(barrier, devices - 1)
+
+    def send(d, carry):
+        to = (me + d) % devices
+        pltpu.make_async_remote_copy(
+            src_ref=grads,
+            dst_ref=grads_out.at[me],
+            send_sem=sems.at[0],
+            recv_sem=sems.at[1],
+            device_id=peer_of(to, copies),
+            device_id_type=pl.DeviceIdType.MESH,
+        ).start()
+        pltpu.make_async_remote_copy(
+            src_ref=conv.at[to],
+            dst_ref=conv_out.at[me],
+            send_sem=sems.at[2],
+            recv_sem=sems.at[3],
+            device_id=peer_of(to, copies),
+            device_id_type=pl.DeviceIdType.MESH,
+        ).start()
+        return carry
+
+    lax.fori_loop(1, devices, send, 0)
+    keep = pltpu.make_async_copy(conv.at[me], conv_out.at[me], sems.at[4])
+    keep.start()
+    grads_out[me] = grads[...]
+    keep.wait()
+    others = pl.ds(0, devices - 1)
+    for sem in (0, 1):
+        pltpu.make_async_copy(grads_out.at[others], grads_out.at[others], sems.at[sem]).wait()
+    for sem in (2, 3):
+        pltpu.make_async_copy(conv_out.at[others], conv_out.at[others], sems.at[sem]).wait()
+
+
+def exchange(devices, copies, conv, grads):
+    return pl.pallas_call(
+        lambda *refs: exchange_kernel(devices, copies, *refs),
+        out_shape=(
+            jax.ShapeDtypeStruct(conv.shape, conv.dtype),
+            jax.ShapeDtypeStruct((devices,) + grads.shape, grads.dtype),
+        ),
+        in_specs=[pl.BlockSpec(memory_space=pltpu.VMEM)] * 2,
+        out_specs=[pl.BlockSpec(memory_space=pltpu.VMEM)] * 2,
+        scratch_shapes=[pltpu.SemaphoreType.DMA((5,))],
+        compiler_params=pltpu.CompilerParams(
+            collective_id=0, has_side_effects=True, vmem_limit_bytes=48 * 1024 * 1024
+        ),
+        name="exchange",
+    )(conv, grads)
 
 
 def local(inputs, out_grad, log_rate, pole_angle, weight_real, weight_imag, passthrough):
@@ -46,13 +117,14 @@
     n_freq = freq_rows * slice_len
     me = lax.axis_index("seq") * copies + lax.axis_index("batch")
 
-    def to_channels(x):
-        x = x.reshape(batch_rows, slice_len, devices, own_ch).transpose(2, 0, 3, 1)
-        x = lax.all_to_all(x, AXES, split_axis=0, concat_axis=0, tiled=True)
-        return x.reshape(rows, batch, own_ch, slice_len)
-
-    grad_cols = to_channels(out_grad)
-    in_cols = to_channels(inputs)
+    def to_parts(x):
+        x = x.reshape(batch_rows, slice_len, devices, own_ch)
+        return x.transpose(2, 0, 3, 1).reshape(devices, 1, batch_rows * own_ch, slice_len)
+
+    both = jnp.concatenate([to_parts(out_grad), to_parts(inputs)], axis=1)
+    both = lax.all_to_all(both, AXES, split_axis=0, concat_axis=0, tiled=True)
+    grad_cols = both[:, 0].reshape(rows, batch, own_ch, slice_len)
+    in_cols = both[:, 1].reshape(rows, batch, own_ch, slice_len)
 
     k_index = jnp.arange(half, dtype=jnp.int32)
     r_index = jnp.arange(freq_rows, dtype=jnp.int32)
@@ -121,12 +193,7 @@
     back = jnp.einsum("kbxc,kac->kbxa", prod, two16, preferred_element_type=jnp.float32)
     back = back.astype(jnp.bfloat16).reshape(half, batch, own_ch, 2, slice_len)
     conv = jnp.einsum("kir,kbxim->rbxm", back16[:, :, :rows], back, preferred_element_type=jnp.float32)
-    conv = conv.astype(jnp.bfloat16).reshape(devices, batch_rows, own_ch, slice_len)
-    conv = lax.all_to_all(conv, AXES, split_axis=0, concat_axis=0, tiled=True)
-    conv = conv.transpose(1, 3, 0, 2).reshape(batch_rows, slice_len, channels)
-    input_grad = (conv.astype(jnp.float32) + passthrough * out_grad.astype(jnp.float32)).astype(
-        jnp.bfloat16
-    )
+    conv = conv.astype(jnp.bfloat16).reshape(devices, batch_rows * own_ch, slice_len)
 
     in_real, in_imag = forward(in_cols)
     cross = jnp.concatenate(
@@ -173,8 +240,17 @@
     pass_part = jnp.sum(
         in_cols.astype(jnp.float32) * grad_cols.astype(jnp.float32), axis=(0, 1, 3)
     )
-    packed = jnp.concatenate([rate_grad, angle_grad, wr_grad, wi_grad, jnp.broadcast_to(pass_part[:, None], rate.shape)], axis=1)
-    packed = lax.all_gather(packed, AXES, axis=0, tiled=True)
+    pass_cols = jnp.broadcast_to(pass_part[:, None], rate.shape)
+    packed = jnp.concatenate(
+        [rate_grad, angle_grad, wr_grad, wi_grad, pass_cols, pass_cols], axis=1
+    )
+    conv, packed = exchange(devices, copies, conv, packed)
+    packed = packed.reshape(channels, -1)
+    conv = conv.reshape(devices, batch_rows, own_ch, slice_len)
+    conv = conv.transpose(1, 3, 0, 2).reshape(batch_rows, slice_len, channels)
+    input_grad = (conv.astype(jnp.float32) + passthrough * out_grad.astype(jnp.float32)).astype(
+        jnp.bfloat16
+    )
     return (
         input_grad,
         packed[:, :states],

time: 132 us -> 109 us (0.83)
  the two profiles are of different devices: /device:TPU:0 before, /device:TPU:15 now
where the time goes in v2:
time: 109 us; the launch traced here: 108 us
  Pallas kernels  37.5 us (34%)
  local copies, waits for them, and re-layouts  22.4 us (21%)
  matrix products  17.6 us (16%)
  other arithmetic  14.3 us (13%)
  waiting for transfers between devices  9.42 us (9%)
  starting transfers between devices  6.28 us (6%)
    pallas_call x1, Pallas kernels, exchange(): pl.pallas_call(lambda *refs: exchange_kernel(devices, copies, *refs), out...  37.5 us
    unnamed x46, local copies, waits for them, and re-layouts  10.7 us
    all_to_all x1, waiting for transfers between devices, local(): both = lax.all_to_all(both, AXES, split_axis=0, concat_axis=0, tiled=True)  9.42 us
    all_to_all x1, starting transfers between devices, local(): both = lax.all_to_all(both, AXES, split_axis=0, concat_axis=0, tiled=True)  6.28 us
    mul x1, other arithmetic, local(): steps * fine[0]  3.86 us
    dot_general x2, matrix products, forward(): jnp.einsum('kbxa,kac->kbxc', g, two16, preferred_element_type=jnp.float32)  3.67 us
    dot_general x1, matrix products, local(): jnp.einsum('xsm,xrm->xsr', jnp.concatenate([fine[0], fine[1], steps * fin...  3.27 us
    reshape x2, local copies, waits for them, and re-layouts, forward(): g = g.astype(jnp.bfloat16).reshape(half, batch, own_ch, 2 * slice_len)  3.13 us
  transfers between devices with their start and end apart: 1, of which 1 were waited for; matrix products, arithmetic and copies ran while one was open for 13% of the time, Pallas kernels for 0%

profile of v2, /device:TPU:15, one launch (start us, length us, event | category | flops | bytes accessed | tf_op | source)
XLA Modules:
  0.0 108.5 jit_solution(1338035110357727654)
XLA Ops:
  0.6 1.4 %copy.109 = bf16[4,128,512]{1,2,0:T(8,128)(2,1)S(1)} copy(bf16[4,128,512]{2,1,0:T(8,128)(2,1)} %param.8) | data formatting | bytes 1048576 | tf_op args[1]
  3.0 1.1 copy.113
  4.1 6.3 %all-to-all-start = ((bf16[32,2,64,128]{3,2,1,0:T(8,128)(2,1)}), bf16[32,2,64,128]{3,2,1,0:T(8,128)(2,1)S(1)}, u32[]{:S(2)}, u32[]{:S(2)}) async-start(bf16[32,2,64,128]{3,2,1,0:T(8,128)(2,1)} %copy.113), calls=%async_computation | async-start | bytes 2097152 | tf_op jit(solution)/shard_map/all_to_all | solution.py:125
  10.4 0.9 constant_dynamic-slice_fusion.2
  11.2 0.9 constant_dynamic-slice_fusion
  12.8 3.9 %iota_multiply_fusion.1 = (f32[16,64,128]{1,0,2:T(8,128)S(1)}, f32[16,64,128]{1,0,2:T(8,128)S(1)}, f32[16,64,128]{1,0,2:T(8,128)S(1)}, f32[16,64,128]{1,0,2:T(8,128)S(1)}) fusion(f32[16,64]{1,0:T(8,128)S(1)} %get-tuple-element.77, f32[16,64]{1,0:T(8,128)S(1)} %get-tuple-element.75), kind=kLoop, calls=%fused_computation.40 | loop fusion | flops 786432 | bytes 2105344 | tf_op jit(solution)/shard_map/mul | solution.py:213
  16.7 1.4 %pad_maximum_fusion.1 = f32[16,128,128]{1,0,2:T(8,128)} fusion(f32[16,64,128]{1,0,2:T(8,128)S(1)} %get-tuple-element.70, f32[16,64,128]{1,0,2:T(8,128)S(1)} %get-tuple-element.71), kind=kLoop, calls=%fused_computation.33 | loop fusion | flops 262144 | bytes 2097152 | tf_op jit(solution)/shard_map/concatenate | solution.py:173
  18.1 2.2 %pad_maximum_fusion = f32[16,256,128]{1,0,2:T(8,128)} fusion(f32[16,64,128]{1,0,2:T(8,128)S(1)} %get-tuple-element.69, f32[16,64,128]{1,0,2:T(8,128)S(1)} %get-tuple-element.68, f32[16,64,128]{1,0,2:T(8,128)S(1)} %get-tuple-element.70, f32[16,64,128]{1,0,2:T(8,128)S(1)} %get-tuple-element.71), kind=kLoop, calls=%fused_computation.7 | loop fusion | flops 1572864 | bytes 4194304 | tf_op jit(solution)/shard_map/concatenate | solution.py:213
  20.3 1.7 %cosine_multiply_fusion.1 = (f32[16,64,33]{1,0,2:T(8,128)S(1)}, f32[16,64,33]{1,0,2:T(8,128)}) fusion(f32[16,64]{1,0:T(8,128)S(1)} %get-tuple-element.76, f32[16,64]{1,0:T(8,128)S(1)} %get-tuple-element.74), kind=kLoop, calls=%fused_computation.53 | loop fusion | flops 135168 | bytes 278528 | tf_op jit(solution)/shard_map/mul | solution.py:36
  22.0 2.1 %fusion.38 = (f32[17,128,128]{2,1,0:T(8,128)}, f32[17,128,128]{2,1,0:T(8,128)}, f32[17,128,128]{2,1,0:T(8,128)}) fusion(f32[128,128]{1,0:T(8,128)S(1)} %get-tuple-element.80, f32[17,128]{1,0:T(8,128)S(1)} %get-tuple-element.83, f32[128,128]{1,0:T(8,128)S(1)} %get-tuple-element.81, f32[17,128]{1,0:T(8,128)S(1)} %get-tuple-element.82), kind=kLoop, calls=%fused_computation.67 | loop fusion | flops 1949696 | bytes 3490816 | tf_op jit(solution)/shard_map/neg | solution.py:140
  24.0 9.4 %all-to-all-done = bf16[32,2,64,128]{3,2,1,0:T(8,128)(2,1)S(1)} async-done(((bf16[32,2,64,128]{3,2,1,0:T(8,128)(2,1)}), bf16[32,2,64,128]{3,2,1,0:T(8,128)(2,1)S(1)}, u32[]{:S(2)}, u32[]{:S(2)}) %all-to-all-start) | async-done | bytes 1048608 | tf_op jit(solution)/shard_map/all_to_all | solution.py:125
  34.5 0.9 fusion.100
  36.0 1.1 %copy.117 = bf16[17,8,16,2,128]{4,3,2,1,0:T(2,128)(2,1)S(1)} copy(bf16[17,8,16,2,128]{4,0,3,2,1:T(8,128)(2,1)S(1)} %fusion.16) | data formatting | bytes 2228224 | tf_op jit(solution)/shard_map/convert_element_type | solution.py:183
  37.1 1.5 %reshape.243 = bf16[17,8,16,256]{3,2,1,0:T(8,128)(2,1)} reshape(bf16[17,8,16,2,128]{4,3,2,1,0:T(2,128)(2,1)S(1)} %copy.117) | data formatting | bytes 2228224 | tf_op jit(solution)/shard_map/reshape | solution.py:183
  38.6 1.6 %fusion.17 = bf16[17,8,16,2,128]{4,0,3,2,1:T(8,128)(2,1)S(1)} fusion(bf16[16,8,16,128,1]{3,2,1,0,4:T(8,128)(2,1)} %bitcast.251, f32[17,1,32]{2,0,1:T(8,128)S(1)} %get-tuple-element.79, f32[17,1,32]{2,0,1:T(8,128)S(1)} %get-tuple-element.78), kind=kOutput, calls=%fused_computation.19 | convolution fusion | flops 18385024 | bytes 1642752 | tf_op jit(solution)/shard_map/kir,rbxm->kbxim/dot_general | solution.py:182
  40.3 1.1 %copy.124 = bf16[17,8,16,2,128]{4,3,2,1,0:T(2,128)(2,1)S(1)} copy(bf16[17,8,16,2,128]{4,0,3,2,1:T(8,128)(2,1)S(1)} %fusion.17) | data formatting | bytes 2228224 | tf_op jit(solution)/shard_map/convert_element_type | solution.py:183
  41.4 1.6 %reshape.246 = bf16[17,8,16,256]{3,2,1,0:T(8,128)(2,1)} reshape(bf16[17,8,16,2,128]{4,3,2,1,0:T(2,128)(2,1)S(1)} %copy.124) | data formatting | bytes 2228224 | tf_op jit(solution)/shard_map/reshape | solution.py:183
  43.0 3.2 %fusion.4 = f32[17,8,16,256]{3,2,1,0:T(8,128)S(1)} fusion(bf16[17,8,16,256]{3,2,1,0:T(8,128)(2,1)} %reshape.243, f32[17,128,128]{2,1,0:T(8,128)} %get-tuple-element.65, f32[17,128,128]{2,1,0:T(8,128)} %get-tuple-element.64, f32[17,128,128]{2,1,0:T(8,128)} %get-tuple-element.63), kind=kOutput, calls=%fused_computation.5 | convolution fusion | flops 294125568 | bytes 6684672 | tf_op jit(solution)/shard_map/kbxa,kac->kbxc/dot_general | solution.py:184
  47.3 0.9 copy-done
  48.6 2.0 %fusion.8 = f32[17,16,256]{2,1,0:T(8,128)S(1)} fusion(f32[17,128,128]{2,1,0:T(8,128)S(1)} %copy-done.12, f32[17,128,128]{2,1,0:T(8,128)S(1)} %copy-done.9, f32[17,128,128]{2,1,0:T(8,128)S(1)} %copy-done.7, f32[17,16,128]{2,1,0:T(8,128)S(1)} %get-tuple-element.29, f32[17,16,128]{2,1,0:T(8,128)S(1)} %get-tuple-element.28), kind=kOutput, calls=%fused_computation.10 | convolution fusion | flops 110366720 | bytes 3899392 | tf_op jit(solution)/shard_map/kxc,kac->kxa/dot_general | solution.py:206
  51.3 3.3 %fusion.6 = f32[16,256,32]{1,2,0:T(8,128)S(1)} fusion(f32[16,256,128]{1,0,2:T(8,128)} %pad_maximum_fusion, f32[16,128,32,1]{1,2,3,0:T(8,128)S(1)} %fusion.31), kind=kOutput, calls=%fused_computation.8 | convolution fusion | flops 100663296 | bytes 2883584 | tf_op jit(solution)/shard_map/xsm,xrm->xsr/dot_general | solution.py:211
  56.8 1.1 %convolution_bitcast_fusion.1 = f32[32,16,128,1]{2,0,3,1:T(8,128)S(1)} fusion(f32[16,128,128]{1,0,2:T(8,128)S(1)} %copy-done.4, f32[16,128,32]{1,0,2:T(8,128)S(1)} %pad_maximum_fusion.3), kind=kOutput, calls=%fused_computation.23 | convolution fusion | flops 50331648 | bytes 1572864 | tf_op jit(solution)/shard_map/xsr,xsm->rxm/dot_general | solution.py:170
  58.6 3.0 %fusion.10 = f32[17,16,256]{2,1,0:T(8,128)S(1)} fusion(f32[17,16,256]{2,1,0:T(8,128)S(1)} %reshape.238, f32[17,128,128]{2,1,0:T(8,128)} %get-tuple-element.65, f32[17,128,128]{2,1,0:T(8,128)S(1)} %copy-done.10, f32[17,128,128]{2,1,0:T(8,128)S(1)} %copy-done.8), kind=kOutput, calls=%fused_computation.12 | convolution fusion | flops 110297088 | bytes 3899392 | tf_op jit(solution)/shard_map/kxa,kab->kxb/dot_general | solution.py:177
  62.1 0.8 copy-done.11
  63.3 0.9 fusion.13
  64.5 0.8 fusion.21
  65.6 37.5 %exchange.1 = (bf16[32,64,128]{2,1,0:T(8,128)(2,1)S(1)}, f32[32,16,384]{2,1,0:T(8,128)S(1)}) custom-call(bf16[32,64,128]{2,1,0:T(8,128)(2,1)S(1)} %bitcast.245, f32[16,384]{1,0:T(8,128)S(1)} %concatenate.40.refs_1_), custom_call_target="tpu_custom_call" | custom-call | tf_op jit(solution)/shard_map/exchange/pallas_call | solution.py:92
  104.1 0.8 copy.168
  104.8 0.8 copy.167
  105.6 0.8 copy.166
  106.4 0.8 copy.165
  107.5 1.0 copy.138
  (78 shorter events, 11.1 us)
Async XLA Ops:
  0.6 1.5 %copy-start.14 = (bf16[4,128,512]{2,1,0:T(8,128)(2,1)S(1)}, bf16[4,128,512]{2,1,0:T(8,128)(2,1)}, u32[]{:S(2)}) copy-start(bf16[4,128,512]{2,1,0:T(8,128)(2,1)} %param.7) | copy-start | bytes 1572868
  2.0 0.9 copy-start.2
  4.1 29.4 %all-to-all-start = ((bf16[32,2,64,128]{3,2,1,0:T(8,128)(2,1)}), bf16[32,2,64,128]{3,2,1,0:T(8,128)(2,1)S(1)}, u32[]{:S(2)}, u32[]{:S(2)}) async-start(bf16[32,2,64,128]{3,2,1,0:T(8,128)(2,1)} %copy.113), calls=%async_computation | async-start | bytes 2097152 | tf_op jit(solution)/shard_map/all_to_all | solution.py:125
  43.0 3.2 %copy-start.6 = (bf16[17,8,16,256]{3,2,1,0:T(8,128)(2,1)S(1)}, bf16[17,8,16,256]{3,2,1,0:T(8,128)(2,1)}, u32[]{:S(2)}) copy-start(bf16[17,8,16,256]{3,2,1,0:T(8,128)(2,1)} %reshape.246) | copy-start | bytes 3342340
  43.0 3.2 %copy-start.7 = (f32[17,128,128]{2,1,0:T(8,128)S(1)}, f32[17,128,128]{2,1,0:T(8,128)}, u32[]{:S(2)}) copy-start(f32[17,128,128]{2,1,0:T(8,128)} %get-tuple-element.63) | copy-start | bytes 3342340
  43.0 3.6 %copy-start.9 = (f32[17,128,128]{2,1,0:T(8,128)S(1)}, f32[17,128,128]{2,1,0:T(8,128)}, u32[]{:S(2)}) copy-start(f32[17,128,128]{2,1,0:T(8,128)} %get-tuple-element.64) | copy-start | bytes 3342340
  43.0 3.9 %copy-start.12 = (f32[17,128,128]{2,1,0:T(8,128)S(1)}, f32[17,128,128]{2,1,0:T(8,128)}, u32[]{:S(2)}) copy-start(f32[17,128,128]{2,1,0:T(8,128)} %get-tuple-element.65) | copy-start | bytes 3342340
  46.9 1.4 %copy-start = (f32[17,8,16,256]{3,2,1,0:T(8,128)}, f32[17,8,16,256]{3,2,1,0:T(8,128)S(1)}, u32[]{:S(2)}) copy-start(f32[17,8,16,256]{3,2,1,0:T(8,128)S(1)} %fusion.4) | copy-start | bytes 6684676
  54.6 1.0 copy-start.5
  55.6 1.2 %copy-start.4 = (f32[16,128,128]{1,0,2:T(8,128)S(1)}, f32[16,128,128]{1,0,2:T(8,128)}, u32[]{:S(2)}) copy-start(f32[16,128,128]{1,0,2:T(8,128)} %pad_maximum_fusion.1) | copy-start | bytes 3145732
  56.8 1.8 %copy-start.8 = (f32[17,128,128]{2,1,0:T(8,128)S(1)}, f32[17,128,128]{2,1,0:T(8,128)}, u32[]{:S(2)}) copy-start(f32[17,128,128]{2,1,0:T(8,128)} %get-tuple-element.63) | copy-start | bytes 3342340
  56.8 1.8 %copy-start.10 = (f32[17,128,128]{2,1,0:T(8,128)S(1)}, f32[17,128,128]{2,1,0:T(8,128)}, u32[]{:S(2)}) copy-start(f32[17,128,128]{2,1,0:T(8,128)} %get-tuple-element.64) | copy-start | bytes 3342340
  58.6 3.1 %copy-start.1 = (f32[17,8,16,256]{3,2,1,0:T(8,128)S(1)}, f32[17,8,16,256]{3,2,1,0:T(8,128)}, u32[]{:S(2)}) copy-start(f32[17,8,16,256]{3,2,1,0:T(8,128)} %copy-done) | copy-start | bytes 6684676
  61.7 1.2 %copy-start.11 = (f32[17,128,128]{2,1,0:T(8,128)S(1)}, f32[17,128,128]{2,1,0:T(8,128)}, u32[]{:S(2)}) copy-start(f32[17,128,128]{2,1,0:T(8,128)} %get-tuple-element.64) | copy-start | bytes 3342340
  61.7 1.6 %copy-start.13 = (f32[17,128,128]{2,1,0:T(8,128)S(1)}, f32[17,128,128]{2,1,0:T(8,128)}, u32[]{:S(2)}) copy-start(f32[17,128,128]{2,1,0:T(8,128)} %get-tuple-element.65) | copy-start | bytes 3342340
  64.5 1.0 copy-start.15
  104.1 3.2 %copy-start.3 = (bf16[4,128,512]{1,2,0:T(8,128)(2,1)S(1)}, bf16[4,128,512]{1,2,0:T(8,128)(2,1)}, u32[]{:S(2)}) copy-start(bf16[4,128,512]{1,2,0:T(8,128)(2,1)} %copy-done.2) | copy-start | bytes 1572868
  104.1 3.2 %copy-start.16 = (f32[512]{0:T(512)S(1)}, f32[512]{0:T(512)}, u32[]{:S(2)}) copy-start(f32[512]{0:T(512)} %param.13) | copy-start | bytes 6148

commit v3 on v2

v3 whole, which is shorter than its diff:
```python
import math

import jax
import jax.numpy as jnp
from jax import lax
from jax.experimental import pallas as pl
from jax.experimental.pallas import tpu as pltpu
from jax.sharding import PartitionSpec as P

TWO_PI = 2.0 * math.pi
AXES = ("seq", "batch")
HIGH = lax.Precision.HIGH


def cos_sin(numerator, length):
    phases = (numerator % length).astype(jnp.float32) * (TWO_PI / length)
    return (jnp.cos(phases), jnp.sin(phases))


def cmul(a, b):
    return (a[0] * b[0] - a[1] * b[1], a[0] * b[1] + a[1] * b[0])


def cdiv(a, b):
    inv = 1.0 / (b[0] * b[0] + b[1] * b[1])
    return ((a[0] * b[0] + a[1] * b[1]) * inv, (a[1] * b[0] - a[0] * b[1]) * inv)


def powers(rate, angle, step, counts):
    turn = angle * step
    laps = jnp.round(turn * (1.0 / TWO_PI))
    turn = (turn - laps * 6.28125) - laps * (TWO_PI - 6.28125)
    n = counts.astype(jnp.float32)
    size = jnp.exp(-(rate * step)[..., None] * n)
    phase = turn[..., None] * n
    return (size * jnp.cos(phase), size * jnp.sin(phase))


def peer_of(place, copies):
    return {"seq": place // copies, "batch": place % copies}


def nt_dot(left, right):
    return lax.dot_general(
        left, right, (((1,), (1,)), ((), ())), preferred_element_type=jnp.float32
    )


def split_dot(values, table):
    high = values.astype(jnp.bfloat16).astype(jnp.float32)
    low = values - high
    count = values.shape[0]
    if count % 8 == 0:
        both = jnp.concatenate([high, low], axis=0).astype(jnp.bfloat16)
        both = nt_dot(both, table)
        return both[:count] + both[count:]
    return nt_dot(high.astype(jnp.bfloat16), table) + nt_dot(low.astype(jnp.bfloat16), table)


def middle_kernel(
    copies, own_ch, one, back_one, corr_one, x, kern, two, fine, coarse,
    conv_out, sums_out, wide, spec, back, conv, corr_part, corr, passed, pay, sems,
):
    devices, _, part, width = x.shape
    rows = devices // copies
    half = rows + 1
    freq_rows = 2 * rows
    cols = copies * part
    me = lax.axis_index("seq") * copies + lax.axis_index("batch")
    barrier = pltpu.get_barrier_semaphore()

    def greet(d, carry):
        pl.semaphore_signal(
            barrier,
            inc=1,
            device_id=peer_of((me + d) % devices, copies),
            device_id_type=pl.DeviceIdType.MESH,
        )
        return carry

    lax.fori_loop(1, devices, greet, 0)

    def over_batch(values):
        if own_ch % 8 == 0:
            return jnp.sum(values.reshape(cols // own_ch, own_ch, -1), axis=0)
        pick = lax.broadcasted_iota(jnp.int32, (own_ch, cols), 1) % own_ch
        pick = pick == lax.broadcasted_iota(jnp.int32, (own_ch, cols), 0)
        return jnp.dot(
            pick.astype(jnp.float32), values, precision=lax.Precision.HIGHEST,
            preferred_element_type=jnp.float32,
        )

    def widen(signal):
        def one_row(r, carry):
            for c in range(copies):
                wide[r, c * part : (c + 1) * part] = x[r * copies + c, signal].astype(jnp.float32)
            return carry

        lax.fori_loop(0, rows, one_row, 0)

    def spectrum(k):
        def add(r, sums):
            value = wide[r]
            return (sums[0] + one[2 * k, r] * value, sums[1] + one[2 * k + 1, r] * value)

        zero = jnp.zeros((cols, width), jnp.float32)
        g = lax.fori_loop(0, rows, add, (zero, zero), unroll=min(rows, 16))
        g = jnp.concatenate(g, axis=1).astype(jnp.bfloat16)
        return jnp.dot(g, two[k], preferred_element_type=jnp.float32)

    widen(0)

    def out_step(k, carry):
        s = spectrum(k)
        spec[k] = s
        kk = kern[k]
        if own_ch % 8 == 0:
            kk = jnp.broadcast_to(kk[None], (cols // own_ch,) + kk.shape).reshape(cols, 2 * width)
        sr, si, kr, ki = s[:, :width], s[:, width:], kk[:, :width], kk[:, width:]
        prod = jnp.concatenate([kr * sr + ki * si, kr * si - ki * sr], axis=1)
        back[k] = nt_dot(prod.astype(jnp.bfloat16), two[k])
        return carry

    lax.fori_loop(0, half, out_step, 0)

    def conv_step(r, carry):
        def add(k, total):
            value = back[k]
            return (
                total + back_one[2 * k, r] * value[:, :width]
                + back_one[2 * k + 1, r] * value[:, width:]
            )

        total = lax.fori_loop(
            0, half, add, jnp.zeros((cols, width), jnp.float32), unroll=half if half < 20 else 1
        )
        total = total.astype(jnp.bfloat16)
        for c in range(copies):
            conv[r * copies + c] = total[c * part : (c + 1) * part]
        return carry

    lax.fori_loop(0, rows, conv_step, 0)
    pl.semaphore_wait(barrier, devices - 1)

    def send_conv(d, carry):
        to = (me + d) % devices
        pltpu.make_async_remote_copy(
            src_ref=conv.at[to],
            dst_ref=conv_out.at[me],
            send_sem=sems.at[2],
            recv_sem=sems.at[3],
            device_id=peer_of(to, copies),
            device_id_type=pl.DeviceIdType.MESH,
        ).start()
        return carry

    lax.fori_loop(1, devices, send_conv, 0)
    keep = pltpu.make_async_copy(conv.at[me], conv_out.at[me], sems.at[4])
    keep.start()

    passed[...] = jnp.zeros_like(passed)

    def pass_step(r, carry):
        passed[...] += jnp.concatenate(
            [
                x[r * copies + c, 1].astype(jnp.float32) * wide[r, c * part : (c + 1) * part]
                for c in range(copies)
            ],
            axis=0,
        )
        return carry

    lax.fori_loop(0, rows, pass_step, 0)
    widen(1)

    def in_step(k, carry):
        s = spectrum(k)
        o = spec[k]
        ir, ii, outr, outi = s[:, :width], s[:, width:], o[:, :width], o[:, width:]
        cross = jnp.concatenate([outr * ir + outi * ii, outi * ir - outr * ii], axis=1)
        corr_part[k] = split_dot(over_batch(cross), two[k])
        return carry

    lax.fori_loop(0, half, in_step, 0)

    def corr_step(r, carry):
        def add(k, total):
            value = corr_part[k]
            return (
                total + corr_one[2 * k, r] * value[:, :width]
                + corr_one[2 * k + 1, r] * value[:, width:]
            )

        corr[r] = lax.fori_loop(
            0, half, add, jnp.zeros((own_ch, width), jnp.float32), unroll=half if half < 20 else 1
        )
        return carry

    lax.fori_loop(0, freq_rows, corr_step, 0)
    states = fine.shape[1] // 4
    far = lax.broadcasted_iota(jnp.int32, (freq_rows, 2 * states), 0).astype(jnp.float32) * width
    first = lax.broadcasted_iota(jnp.int32, (freq_rows, 2 * states), 1) < states
    sign = jnp.where(first, -1.0, 1.0).astype(jnp.float32)
    for c in range(own_ch):
        low = split_dot(corr[:, c, :], fine[c])
        base = low[:, : 2 * states]
        step = far * base + low[:, 2 * states :]
        for i, value in enumerate((base, step)):
            turned = pltpu.roll(value, states, 1) * sign
            total = jnp.sum(coarse[c, 0] * value + coarse[c, 1] * turned, axis=0, keepdims=True)
            pay[c : c + 1, 2 * states * i : 2 * states * (i + 1)] = total
    products = jnp.sum(over_batch(passed[...]), axis=1, keepdims=True)
    lane = lax.broadcasted_iota(jnp.int32, (own_ch, width), 1)
    pay[:, 4 * states :] = jnp.where(lane == 0, corr[0], products)

    def send_sums(d, carry):
        to = (me + d) % devices
        pltpu.make_async_remote_copy(
            src_ref=pay,
            dst_ref=sums_out.at[me],
            send_sem=sems.at[0],
            recv_sem=sems.at[1],
            device_id=peer_of(to, copies),
            device_id_type=pl.DeviceIdType.MESH,
        ).start()
        return carry

    lax.fori_loop(1, devices, send_sums, 0)
    sums_out[me] = pay[...]
    keep.wait()
    others = pl.ds(0, devices - 1)
    for sem in (2, 3):
        pltpu.make_async_copy(conv_out.at[others], conv_out.at[others], sems.at[sem]).wait()
    for sem in (0, 1):
        pltpu.make_async_copy(sums_out.at[others], sums_out.at[others], sems.at[sem]).wait()


def middle(copies, own_ch, one, back_one, corr_one, x, kern, two, fine, coarse):
    devices, _, part, width = x.shape
    rows = devices // copies
    half = rows + 1
    cols = copies * part
    lanes = fine.shape[1] + width
    vmem = pl.BlockSpec(memory_space=pltpu.VMEM)
    smem = pl.BlockSpec(memory_space=pltpu.SMEM)
    f32 = jnp.float32
    return pl.pallas_call(
        lambda *refs: middle_kernel(copies, own_ch, *refs),
        out_shape=(
            jax.ShapeDtypeStruct((devices, part, width), jnp.bfloat16),
            jax.ShapeDtypeStruct((devices, own_ch, lanes), f32),
        ),
        in_specs=[smem] * 3 + [vmem] * 5,
        out_specs=[vmem] * 2,
        scratch_shapes=[
            pltpu.VMEM((rows, cols, width), f32),
            pltpu.VMEM((half, cols, 2 * width), f32),
            pltpu.VMEM((half, cols, 2 * width), f32),
            pltpu.VMEM((devices, part, width), jnp.bfloat16),
            pltpu.VMEM((half, own_ch, 2 * width), f32),
            pltpu.VMEM((2 * rows, own_ch, width), f32),
            pltpu.VMEM((cols, width), f32),
            pltpu.VMEM((own_ch, lanes), f32),
            pltpu.SemaphoreType.DMA((5,)),
        ],
        compiler_params=pltpu.CompilerParams(
            collective_id=0, has_side_effects=True, vmem_limit_bytes=52 * 1024 * 1024
        ),
        name="middle",
    )(one, back_one, corr_one, x, kern, two, fine, coarse)


def local(inputs, out_grad, log_rate, pole_angle, weight_real, weight_imag, passthrough):
    batch_rows, slice_len, channels = inputs.shape
    rows = lax.axis_size("seq")
    copies = lax.axis_size("batch")
    devices = rows * copies
    own_ch = channels // devices
    batch = batch_rows * copies
    freq_rows = 2 * rows
    half = rows + 1
    n_freq = freq_rows * slice_len
    me = lax.axis_index("seq") * copies + lax.axis_index("batch")

    def to_parts(x):
        x = x.reshape(batch_rows, slice_len, devices, own_ch)
        return x.transpose(2, 0, 3, 1).reshape(devices, 1, batch_rows * own_ch, slice_len)

    both = jnp.concatenate([to_parts(out_grad), to_parts(inputs)], axis=1)
    both = lax.all_to_all(both, AXES, split_axis=0, concat_axis=0, tiled=True)
    k_index = jnp.arange(half, dtype=jnp.int32)
    r_index = jnp.arange(freq_rows, dtype=jnp.int32)
    m_index = jnp.arange(slice_len, dtype=jnp.int32)
    cos_one, sin_one = cos_sin(k_index[:, None] * r_index[None, :], freq_rows)
    table_one = jnp.stack([cos_one, -sin_one], axis=1)
    cos_two, sin_two = cos_sin(m_index[:, None] * m_index[None, :], slice_len)
    turn_real, turn_imag = cos_sin(k_index[:, None] * m_index[None, :], n_freq)
    full_cos = turn_real[:, :, None] * cos_two - turn_imag[:, :, None] * sin_two
    full_sin = turn_imag[:, :, None] * cos_two + turn_real[:, :, None] * sin_two
    table_two = jnp.concatenate(
        [
            jnp.concatenate([full_cos, -full_sin], axis=2),
            jnp.concatenate([full_sin, full_cos], axis=2),
        ],
        axis=1,
    )
    ends = (k_index == 0) | (k_index == rows)
    share = jnp.where(ends, 1.0, 2.0).astype(jnp.float32)[:, None, None] / n_freq
    table_back = table_one * share
    flat = (2 * half, freq_rows)
    held = table_one.astype(jnp.bfloat16).astype(jnp.float32)
    one = held.reshape(flat)
    back_one = (held * (share * n_freq)).reshape(flat)
    corr_one = table_back.reshape(flat)

    def own(p):
        return lax.dynamic_slice_in_dim(p, me * own_ch, own_ch, 0)

    all_rate = jnp.exp(log_rate)
    all_shrink = jnp.sqrt(-jnp.expm1(-2.0 * all_rate))
    rate, angle, shrink = own(all_rate), own(pole_angle), own(all_shrink)
    weight = (own(weight_real) * shrink, own(weight_imag) * shrink)
    fine = powers(rate, angle, 1.0, jnp.arange(slice_len))
    coarse = powers(rate, angle, float(slice_len), jnp.arange(freq_rows))
    whole = tuple(v[..., 0] for v in powers(rate, angle, float(slice_len), jnp.full((1,), freq_rows)))
    lam = (fine[0][..., 1], fine[1][..., 1])
    gap = (1.0 - whole[0], -whole[1])
    bottom = cmul(lam, gap)
    lead = cdiv(weight, bottom)
    tail = 2.0 * jnp.sum(cdiv(weight, lam)[0], axis=1)
    lead_rows = cmul((lead[0][..., None], lead[1][..., None]), coarse)
    taps = jnp.einsum(
        "xsr,xsm->rxm",
        jnp.concatenate([2.0 * lead_rows[0], -2.0 * lead_rows[1]], axis=1),
        jnp.concatenate(fine, axis=1),
        precision=HIGH,
    )
    kern = jnp.einsum("kir,rxm->kxim", table_one, taps, precision=HIGH)
    kern = jnp.einsum("kxa,kab->kxb", kern.reshape(half, own_ch, -1), table_two, precision=HIGH)
    shift = jnp.concatenate([jnp.ones(slice_len), jnp.zeros(slice_len)]).astype(jnp.float32)
    kern = (kern - tail[None, :, None] * shift) / n_freq
    if own_ch % 8:
        kern = jnp.tile(kern, (1, batch, 1))
    steps = jnp.arange(slice_len, dtype=jnp.float32)
    fine = jnp.concatenate([fine[0], fine[1], steps * fine[0], steps * fine[1]], axis=1)
    coarse = jnp.stack([jnp.swapaxes(v, 1, 2) for v in coarse], axis=1)
    conv, packed = middle(
        copies,
        own_ch,
        one,
        back_one,
        corr_one,
        both,
        kern,
        table_two.astype(jnp.bfloat16),
        fine.astype(jnp.bfloat16),
        jnp.concatenate([coarse, coarse], axis=3),
    )
    packed = packed.reshape(channels, -1)
    conv = conv.reshape(devices, batch_rows, own_ch, slice_len)
    conv = conv.transpose(1, 3, 0, 2).reshape(batch_rows, slice_len, channels)
    input_grad = (conv.astype(jnp.float32) + passthrough * out_grad.astype(jnp.float32)).astype(
        jnp.bfloat16
    )

    states = log_rate.shape[1]
    rate, shrink = all_rate, all_shrink
    t0 = (packed[:, :states], packed[:, states : 2 * states])
    t1 = (packed[:, 2 * states : 3 * states], packed[:, 3 * states : 4 * states])
    corr0 = packed[:, 4 * states : 4 * states + 1]
    lam = tuple(v[..., 0] for v in powers(rate, pole_angle, 1.0, jnp.full((1,), 1)))
    whole = tuple(
        v[..., 0] for v in powers(rate, pole_angle, float(slice_len), jnp.full((1,), freq_rows))
    )
    gap = (1.0 - whole[0], -whole[1])
    bottom = cmul(lam, gap)
    weight = (weight_real * shrink, weight_imag * shrink)
    near = cdiv((corr0, jnp.zeros_like(corr0)), lam)
    top = cdiv(t0, bottom)
    h = (top[0] - near[0], top[1] - near[1])
    d = cdiv(t1, bottom)
    ratio = cdiv((1.0 - (n_freq + 1.0) * whole[0], -(n_freq + 1.0) * whole[1]), gap)
    lower = cmul(top, ratio)
    d = (d[0] - lower[0] + near[0], d[1] - lower[1] + near[1])
    wd = cmul(weight, d)
    shrink_part = 2.0 * (weight_real * h[0] - weight_imag * h[1]) * jnp.exp(-2.0 * rate) / shrink
    return (
        input_grad,
        rate * (shrink_part - 2.0 * wd[0]),
        -2.0 * wd[1],
        2.0 * shrink * h[0],
        -2.0 * shrink * h[1],
        packed[:, 4 * states + 1],
    )


def solution(mesh):
    placed = (P("batch", "seq", None), P("batch", "seq", None), P(), P(), P(), P(), P())
    return jax.shard_map(
        local,
        mesh=mesh,
        in_specs=placed,
        out_specs=(P("batch", "seq", None), P(), P(), P(), P(), P()),
        check_vma=False,
    )
```

time: 109 us -> 87.9 us (0.81)
  matrix products: 17.6 us -> 2.15 us
  local copies, waits for them, and re-layouts: 22.4 us -> 11.2 us
  waiting for transfers between devices: 9.42 us -> 0.89 us
  Pallas kernels: 37.5 us -> 45.2 us
  other arithmetic: 14.3 us -> 20.4 us
    dot_general x9 -> x0, matrix products: 13.2 us -> none  [the longest x2 3.67 us: forward(): jnp.einsum('kbxa,kac->kbxc', g, two16, preferred_element_type=jnp.float32)]
    all_to_all x1, waiting for transfers between devices: 9.42 us -> 0.89 us  [local(): both = lax.all_to_all(both, AXES, split_axis=0, concat_axis=0, tiled=True)]
    pallas_call x1, Pallas kernels: 37.5 us -> 45.2 us  [middle(): pl.pallas_call(lambda *refs: middle_kernel(copies, own_ch, *refs), out_sh...]
    unnamed x46 -> x63, local copies, waits for them, and re-layouts: 10.7 us -> 5.01 us
    reshape x4 -> x0, local copies, waits for them, and re-layouts: 3.58 us -> none  [the longest x2 3.13 us: forward(): g = g.astype(jnp.bfloat16).reshape(half, batch, own_ch, 2 * slice_len)]
    another operation x1 -> x2, other arithmetic: 0.39 us -> 3.13 us
    convert_element_type x3 -> x0, local copies, waits for them, and re-layouts: 2.35 us -> none  [the longest x2 2.21 us: forward(): g = g.astype(jnp.bfloat16).reshape(half, batch, own_ch, 2 * slice_len)]
    squeeze x0 -> x2, local copies, waits for them, and re-layouts: none -> 2.19 us  [local(): lam = (fine[0][..., 1], fine[1][..., 1])]
  transfers between devices with their start and end apart: 1 -> 1, of which waited for: 1 -> 1; matrix products, arithmetic and copies ran while one was open for 13% -> 25% of each run, Pallas kernels for 0% -> 0%
where the time goes in v3:
time: 87.9 us; the launch traced here: 87.2 us
  Pallas kernels  45.2 us (51%)
  other arithmetic  20.4 us (23%)
  local copies, waits for them, and re-layouts  11.2 us (13%)
  starting transfers between devices  6.28 us (7%)
  matrix products  2.15 us (2%)
  between operations  1.11 us (1%)
  waiting for transfers between devices  0.89 us (1%)
    pallas_call x1, Pallas kernels, middle(): pl.pallas_call(lambda *refs: middle_kernel(copies, own_ch, *refs), out_sh...  45.2 us
    all_to_all x1, starting transfers between devices, local(): both = lax.all_to_all(both, AXES, split_axis=0, concat_axis=0, tiled=True)  6.28 us
    unnamed x63, local copies, waits for them, and re-layouts  5.01 us
    another operation x1, other arithmetic  3.13 us
    squeeze x2, local copies, waits for them, and re-layouts, local(): lam = (fine[0][..., 1], fine[1][..., 1])  2.19 us
    mul x1, other arithmetic, local(): -2.0 * shrink * h[1]  1.89 us
  transfers between devices with their start and end apart: 1, of which 1 were waited for; matrix products, arithmetic and copies ran while one was open for 25% of the time, Pallas kernels for 0%

profile of v3, /device:TPU:15, one launch (start us, length us, event | category | flops | bytes accessed | tf_op | source)
XLA Modules:
  0.0 87.2 jit_solution(15182123832602317692)
XLA Ops:
  0.6 1.4 %copy.89 = bf16[4,128,512]{1,2,0:T(8,128)(2,1)S(1)} copy(bf16[4,128,512]{2,1,0:T(8,128)(2,1)} %param.8) | data formatting | bytes 1048576 | tf_op args[1]
  2.1 0.3 copy.91
  2.4 1.1 %pad_maximum_fusion = bf16[32,2,64,128]{3,2,1,0:T(8,128)(2,1)} fusion(bf16[32,1,64,128]{3,2,1,0:T(8,128)(2,1)S(1)} %bitcast.76, bf16[32,1,64,128]{3,2,1,0:T(8,128)(2,1)S(1)} %bitcast.75), kind=kLoop, calls=%fused_computation.9 | loop fusion | flops 524288 | bytes 2097152 | tf_op jit(solution)/shard_map/concatenate | solution.py:289
  3.5 6.3 %all-to-all-start = ((bf16[32,2,64,128]{3,2,1,0:T(8,128)(2,1)}), bf16[32,2,64,128]{3,2,1,0:T(8,128)(2,1)S(1)}, u32[]{:S(2)}, u32[]{:S(2)}) async-start(bf16[32,2,64,128]{3,2,1,0:T(8,128)(2,1)} %pad_maximum_fusion), calls=%async_computation | async-start | bytes 2097152 | tf_op jit(solution)/shard_map/all_to_all | solution.py:290
  9.8 0.7 sine_negate_fusion
  10.5 0.9 %fusion.37 = (f32[128,128]{1,0:T(8,128)}, f32[128,128]{1,0:T(8,128)}) fusion(), kind=kLoop, calls=%fused_computation.95 | loop fusion | flops 229376 | bytes 131072 | tf_op jit(solution)/shard_map/sin | solution.py:17
  11.4 0.7 fusion.53
  12.1 0.8 negate_sqrt_fusion
  12.9 0.8 multiply_subtract_fusion.6
  13.8 3.1 %fusion.18 = (bf16[16,64,128]{2,1,0:T(8,128)(2,1)}, bf16[16,64,128]{2,1,0:T(8,128)(2,1)}, bf16[16,64,128]{2,1,0:T(8,128)(2,1)}, bf16[16,64,128]{2,1,0:T(8,128)(2...) fusion(f32[16,64]{1,0:T(8,128)S(1)} %copy.94, f32[128]{0:T(128)S(1)} %iota_convert_fusion.1, ...), kind=kLoop, calls=%fused_computation.40 | loop fusion | flops 1310720 | bytes 2105856 | tf_op jit(solution)/shard_map/convert.3
  17.2 1.1 %copy.122 = f32[16,64,1]{0,1,2:T(8,128)} copy(f32[16,64,1]{2,1,0:T(8,128)S(1)} %slice.32) | data formatting | bytes 8192 | tf_op jit(solution)/shard_map/squeeze | solution.py:326
  18.5 1.1 %copy.123 = f32[16,64,1]{0,1,2:T(8,128)} copy(f32[16,64,1]{2,1,0:T(8,128)S(1)} %slice.33) | data formatting | bytes 8192 | tf_op jit(solution)/shard_map/squeeze | solution.py:326
  19.6 1.4 %fusion.34 = (f32[16]{0:T(128)}, f32[16,64]{0,1:T(8,128)S(1)}, f32[16,64]{0,1:T(8,128)S(1)}) fusion(f32[16,64,1]{0,1,2:T(8,128)} %copy.123, f32[16,64,1]{0,1,2:T(8,128)} %copy.122, f32[512,64]{0,1:T(8,128)} %get-tuple-element.67, s32[]{:T(128)S(6)} %select_n.80, f32[512,64]{0,1:T(8,128)S(1)} %copy-done.7, f32[512,64]{0,1:T(8,128)} %param.11), kind=kLoop, calls=%fused_computation.88 | loop fusion | flops 11248 | bytes 28740 | tf_op jit(solution)/shard_map/reduce_sum | solution.py:330
  21.0 1.0 %fusion.39 = (f32[16,64]{0,1:T(8,128)S(1)}, f32[16,64]{0,1:T(8,128)S(1)}, f32[16,64]{0,1:T(8,128)S(1)}, f32[16,64]{0,1:T(8,128)S(1)}, f32[16,64]{0,1:T(8,128)S(1)}) fusion(f32[16,64]{0,1:T(8,128)S(1)} %get-tuple-element.48, f32[16,64]{0,1:T(8,128)S(1)} %get-tuple-element.49, f32[16,64,1]{0,1,2:T(8,128)} %copy.123, f32[16,64,1]{0,1,2:T(8,128)} %copy.122, ...), kind=kLoop, calls=%fused_computation.99 | loop fusion | flops 29696 | bytes 45060 | tf_op jit(solution)/shard_map/mul | solution.py:26
  22.3 1.1 %subtract_multiply_fusion = (f32[16,64,32]{1,2,0:T(8,128)S(1)}, f32[16,64,32]{1,2,0:T(8,128)S(1)}) fusion(f32[16,64]{1,0:T(8,128)S(1)} %copy.102, f32[16,64]{1,0:T(8,128)S(1)} %copy.101, f32[32]{0:T(128)S(1)} %iota_convert_fusion, f32[16,64]{1,0:T(8,128)S(1)} %copy.100, f32[16,64]{1,0:T(8,128)S(1)} %copy.99), kind=kLoop, calls=%fused_computation.37 | loop fusion | flops 393216 | bytes 278656 | tf_op jit(solution)/shard_map/mul | solution.py:334
  23.5 0.6 convolution_bitcast_fusion.1
  24.1 0.3 convolution_bitcast_fusion
  24.6 0.9 %reshape.302 = f32[17,16,256]{2,1,0:T(8,128)} reshape(f32[17,16,2,128]{3,2,1,0:T(2,128)S(1)} %copy.103) | data formatting | bytes 557056 | tf_op jit(solution)/shard_map/reshape | solution.py:339
  25.9 1.0 %fusion.12 = (f32[16,1,32,64]{3,2,1,0:T(8,128)S(1)}, f32[16,1,32,64]{3,2,1,0:T(8,128)S(1)}) fusion(f32[16,64]{1,0:T(8,128)S(1)} %copy-done.19, f32[32]{0:T(128)S(1)} %copy-done.24, f32[16,64]{1,0:T(8,128)S(1)} %copy-done.17), kind=kLoop, calls=%fused_computation.30 | loop fusion | flops 131072 | bytes 270464 | tf_op jit(solution)/shard_map/mul | solution.py:36
  27.2 1.0 %pad_maximum_fusion.1.refs_6_ = bf16[16,256,128]{2,1,0:T(8,128)(2,1)} fusion(bf16[16,64,128]{2,1,0:T(8,128)(2,1)S(1)} %get-tuple-element.79, bf16[16,64,128]{2,1,0:T(8,128)(2,1)S(1)} %copy-done.5, bf16[16,64,128]{2,1,0:T(8,128)(2,1)S(1)} %copy-done.6, bf16[16,64,128]{2,1,0:T(8,128)(2,1)S(1)} %copy-done.4), kind=kLoop, calls=%fused_computation.13 | loop fusion | flops 4194304 | bytes 2097152 | tf_op jit(solution)/shard_map/concatenate | solution.py:345
  28.3 0.6 fusion.19
  29.0 1.6 %fusion.refs_5_ = bf16[17,256,256]{2,1,0:T(8,128)(2,1)} fusion(f32[17,128,128]{2,1,0:T(8,128)S(1)} %get-tuple-element.66, f32[17,128,128]{2,1,0:T(8,128)S(1)} %get-tuple-element.65, f32[17,128,128]{2,1,0:T(8,128)S(1)} %get-tuple-element.64), kind=kLoop, calls=%fused_computation.1 | loop fusion | flops 8912896 | bytes 5570560 | tf_op jit(solution)/shard_map/convert_element_type | solution.py:355
  30.8 1.3 %fusion.3.refs_4_ = f32[17,16,256]{2,1,0:T(8,128)S(1)} fusion(f32[17,16,256]{2,1,0:T(8,128)S(1)} %copy-done.12, f32[17,128,128]{2,1,0:T(8,128)S(1)} %get-tuple-element.66, f32[17,128,128]{2,1,0:T(8,128)S(1)} %get-tuple-element.65, f32[17,128,128]{2,1,0:T(8,128)S(1)} %get-tuple-element.64, f32[16,256]{1,0:T(8,128)S(1)} %broadcast_multiply_fusion.2), kind=kOutput, calls=%fused_computation.6 | convolution fusion | flops 110436352 | bytes 3915776 | tf_op jit(solution)/shard_map/kxa,kab->kxb/dot_general | solution.py:339
  32.0 0.9 %all-to-all-done.refs_3_ = bf16[32,2,64,128]{3,2,1,0:T(8,128)(2,1)S(1)} async-done(((bf16[32,2,64,128]{3,2,1,0:T(8,128)(2,1)}), bf16[32,2,64,128]{3,2,1,0:T(8,128)(2,1)S(1)}, u32[]{:S(2)}, u32[]{:S(2)}) %all-to-all-start) | async-done | bytes 1048608 | tf_op jit(solution)/shard_map/all_to_all | solution.py:290
  32.9 1.0 %copy-done = bf16[32,2,64,128]{3,2,1,0:T(8,128)(2,1)} copy-done((bf16[32,2,64,128]{3,2,1,0:T(8,128)(2,1)}, bf16[32,2,64,128]{3,2,1,0:T(8,128)(2,1)S(1)}, u32[]{:S(2)}) %copy-start) | copy-done | bytes 1048600
  33.9 45.2 %middle.1 = (bf16[32,64,128]{2,1,0:T(8,128)(2,1)S(1)}, f32[32,16,384]{2,1,0:T(8,128)}) custom-call(f32[34,32]{1,0:T(8,128)S(1)} %get-tuple-element.73.refs_0_, f32[34,32]{1,0:T(8,128)S(1)} %get-tuple-element.72.refs_1_, f32[34,32]{1,0:T(8,128)S(1)} %get-tuple-element.71.refs_2_, bf16[32,2,64,128]{3,2,1,0:T(8,128)(2,1)} %copy-done, ...), custom_call_target="tpu_custom_call" | custom-call | tf_op jit(solution)/shard_map/middle/pallas_call | solution.py:247
  79.1 1.5 %fusion.63 = (f32[512,64]{1,0:T(8,128)S(1)}, f32[512,64]{1,0:T(8,128)S(1)}, f32[512,64]{1,0:T(8,128)S(1)}, f32[512,64]{1,0:T(8,128)S(1)}) fusion(f32[512,384]{1,0:T(8,128)} %bitcast.72), kind=kLoop, calls=%fused_computation.145 | loop fusion | bytes 1048576 | tf_op jit(solution)/shard_map/slice | solution.py:369
  81.7 1.0 %copy.120 = bf16[4,128,512]{2,1,0:T(8,128)(2,1)} copy(bf16[4,128,512]{1,2,0:T(8,128)(2,1)S(1)} %fusion.7) | data formatting | bytes 1048576
  82.7 0.7 copy.129
  83.4 1.9 %multiply_multiply_fusion = (f32[512,64]{0,1:T(8,128)}, f32[512,64]{0,1:T(8,128)S(1)}, f32[512,64]{0,1:T(8,128)S(1)}, f32[512,64]{0,1:T(8,128)S(1)}, f32[512,64]...) fusion(f32[512,64]{0,1:T(8,128)S(1)} %copy-done.3, f32[512]{0:T(512)S(1)} %bitcast.77, ...), kind=kLoop, calls=%fused_computation.42 | loop fusion | flops 1671168 | bytes 1574912 | tf_op jit(solution)/shard_map/mul | solution.py:392
  85.3 1.1 %multiply_multiply_fusion.1 = (f32[512,64]{0,1:T(8,128)}, f32[512,64]{0,1:T(8,128)S(1)}, f32[512,64]{0,1:T(8,128)}, f32[512,64]{0,1:T(8,128)S(1)}, f32[512,64]{0,1:T(8,128)S(1)}) fusion(f32[512,64]{0,1:T(8,128)S(1)} %copy-done.3, f32[512,64]{0,1:T(8,128)S(1)} %get-tuple-element.41, f32[512,64]{0,1:T(8,128)S(1)} %get-tuple-element.40, f32[512]{0:T(512)S(1)} %bitcast.78, ...), kind=kLoop, calls=%fused_computation.43 | loop fusion | flops 2293760 | bytes 2361344 | tf_op jit(solution)/shard_map/mul | solution.py:391
  86.4 0.8 subtract_multiply_fusion.1
  (87 shorter events, 2.9 us)
Async XLA Ops:
  0.6 1.5 %copy-start.9 = (bf16[4,128,512]{2,1,0:T(8,128)(2,1)S(1)}, bf16[4,128,512]{2,1,0:T(8,128)(2,1)}, u32[]{:S(2)}) copy-start(bf16[4,128,512]{2,1,0:T(8,128)(2,1)} %param.7) | copy-start | bytes 1572868
  2.4 9.7 %copy-start.2 = (f32[512,64]{0,1:T(8,128)S(1)}, f32[512,64]{0,1:T(8,128)}, u32[]{:S(2)}) copy-start(f32[512,64]{0,1:T(8,128)} %param.9) | copy-start | bytes 393220
  3.5 29.4 %all-to-all-start = ((bf16[32,2,64,128]{3,2,1,0:T(8,128)(2,1)}), bf16[32,2,64,128]{3,2,1,0:T(8,128)(2,1)S(1)}, u32[]{:S(2)}, u32[]{:S(2)}) async-start(bf16[32,2,64,128]{3,2,1,0:T(8,128)(2,1)} %pad_maximum_fusion), calls=%async_computation | async-start | bytes 2097152 | tf_op jit(solution)/shard_map/all_to_all | solution.py:290
  9.8 12.5 %copy-start.23 = (f32[32]{0:T(128)}, f32[32]{0:T(128)S(1)}, u32[]{:S(2)}) copy-start(f32[32]{0:T(128)S(1)} %iota_convert_fusion) | copy-start | bytes 388
  12.9 0.9 %copy-start.11 = (f32[512,64]{0,1:T(8,128)}, f32[512,64]{0,1:T(8,128)S(1)}, u32[]{:S(2)}) copy-start(f32[512,64]{0,1:T(8,128)S(1)} %get-tuple-element.68) | copy-start | bytes 393220
  17.0 2.6 %copy-start.7 = (f32[512,64]{0,1:T(8,128)S(1)}, f32[512,64]{0,1:T(8,128)}, u32[]{:S(2)}) copy-start(f32[512,64]{0,1:T(8,128)} %param.12) | copy-start | bytes 393220
  19.6 4.6 %copy-start.15 = (f32[17,1,32]{2,0,1:T(8,128)S(1)}, f32[17,1,32]{2,0,1:T(8,128)}, u32[]{:S(2)}) copy-start(f32[17,1,32]{2,0,1:T(8,128)} %get-tuple-element.83) | copy-start | bytes 6532
  22.1 1.4 %copy-start.16 = (f32[16,64]{1,0:T(8,128)}, f32[16,64]{1,0:T(8,128)S(1)}, u32[]{:S(2)}) copy-start(f32[16,64]{1,0:T(8,128)S(1)} %copy.100) | copy-start | bytes 12292
  22.2 1.3 %copy-start.18 = (f32[16,64]{1,0:T(8,128)}, f32[16,64]{1,0:T(8,128)S(1)}, u32[]{:S(2)}) copy-start(f32[16,64]{1,0:T(8,128)S(1)} %copy.101) | copy-start | bytes 12292
  24.1 1.9 %copy-start.17 = (f32[16,64]{1,0:T(8,128)S(1)}, f32[16,64]{1,0:T(8,128)}, u32[]{:S(2)}) copy-start(f32[16,64]{1,0:T(8,128)} %copy-done.16) | copy-start | bytes 12292
  24.1 1.9 %copy-start.19 = (f32[16,64]{1,0:T(8,128)S(1)}, f32[16,64]{1,0:T(8,128)}, u32[]{:S(2)}) copy-start(f32[16,64]{1,0:T(8,128)} %copy-done.18) | copy-start | bytes 12292
  24.1 1.9 %copy-start.24 = (f32[32]{0:T(128)S(1)}, f32[32]{0:T(128)}, u32[]{:S(2)}) copy-start(f32[32]{0:T(128)} %copy-done.23) | copy-start | bytes 388
  24.1 3.1 %copy-start.4 = (bf16[16,64,128]{2,1,0:T(8,128)(2,1)S(1)}, bf16[16,64,128]{2,1,0:T(8,128)(2,1)}, u32[]{:S(2)}) copy-start(bf16[16,64,128]{2,1,0:T(8,128)(2,1)} %get-tuple-element.76) | copy-start | bytes 786436
  24.1 3.1 %copy-start.5 = (bf16[16,64,128]{2,1,0:T(8,128)(2,1)S(1)}, bf16[16,64,128]{2,1,0:T(8,128)(2,1)}, u32[]{:S(2)}) copy-start(bf16[16,64,128]{2,1,0:T(8,128)(2,1)} %get-tuple-element.77) | copy-start | bytes 786436
  24.1 3.1 %copy-start.6 = (bf16[16,64,128]{2,1,0:T(8,128)(2,1)S(1)}, bf16[16,64,128]{2,1,0:T(8,128)(2,1)}, u32[]{:S(2)}) copy-start(bf16[16,64,128]{2,1,0:T(8,128)(2,1)} %get-tuple-element.78) | copy-start | bytes 786436
  25.5 2.7 %copy-start.13 = (f32[128,128]{1,0:T(8,128)S(1)}, f32[128,128]{1,0:T(8,128)}, u32[]{:S(2)}) copy-start(f32[128,128]{1,0:T(8,128)} %get-tuple-element.88) | copy-start | bytes 196612
  25.5 2.7 %copy-start.14 = (f32[128,128]{1,0:T(8,128)S(1)}, f32[128,128]{1,0:T(8,128)}, u32[]{:S(2)}) copy-start(f32[128,128]{1,0:T(8,128)} %get-tuple-element.89) | copy-start | bytes 196612
  25.5 2.7 %copy-start.20 = (f32[17,128]{1,0:T(8,128)S(1)}, f32[17,128]{1,0:T(8,128)}, u32[]{:S(2)}) copy-start(f32[17,128]{1,0:T(8,128)} %get-tuple-element.90) | copy-start | bytes 26116
  25.5 2.7 %copy-start.21 = (f32[17,128]{1,0:T(8,128)S(1)}, f32[17,128]{1,0:T(8,128)}, u32[]{:S(2)}) copy-start(f32[17,128]{1,0:T(8,128)} %get-tuple-element.91) | copy-start | bytes 26116
  28.9 1.7 %copy-start.26 = (f32[16]{0:T(128)S(1)}, f32[16]{0:T(128)}, u32[]{:S(2)}) copy-start(f32[16]{0:T(128)} %get-tuple-element.47) | copy-start | bytes 196
  28.9 1.7 %copy-start.25 = (f32[256]{0:T(256)S(1)}, f32[256]{0:T(256)}, u32[]{:S(2)}) copy-start(f32[256]{0:T(256)} %constant.109.clone.1) | copy-start | bytes 3076
  29.0 1.8 %copy-start.12 = (f32[17,16,256]{2,1,0:T(8,128)S(1)}, f32[17,16,256]{2,1,0:T(8,128)}, u32[]{:S(2)}) copy-start(f32[17,16,256]{2,1,0:T(8,128)} %reshape.302) | copy-start | bytes 835588
  32.9 1.0 %copy-start = (bf16[32,2,64,128]{3,2,1,0:T(8,128)(2,1)}, bf16[32,2,64,128]{3,2,1,0:T(8,128)(2,1)S(1)}, u32[]{:S(2)}) copy-start(bf16[32,2,64,128]{3,2,1,0:T(8,128)(2,1)S(1)} %all-to-all-done.refs_3_) | copy-start | bytes 3145732
  79.1 1.5 %copy-start.1 = (f32[32,16,384]{2,1,0:T(8,128)S(1)}, f32[32,16,384]{2,1,0:T(8,128)}, u32[]{:S(2)}) copy-start(f32[32,16,384]{2,1,0:T(8,128)} %get-tuple-element.9) | copy-start | bytes 2359300
  80.6 0.8 copy-start.22
  81.4 1.9 %copy-start.3 = (f32[512,64]{0,1:T(8,128)S(1)}, f32[512,64]{0,1:T(8,128)}, u32[]{:S(2)}) copy-start(f32[512,64]{0,1:T(8,128)} %param.9) | copy-start | bytes 393220
  81.4 1.9 %copy-start.10 = (f32[512,64]{0,1:T(8,128)S(1)}, f32[512,64]{0,1:T(8,128)}, u32[]{:S(2)}) copy-start(f32[512,64]{0,1:T(8,128)} %param.10) | copy-start | bytes 393220
  81.5 3.8 %copy-start.8 = (f32[512,64]{0,1:T(8,128)S(1)}, f32[512,64]{0,1:T(8,128)}, u32[]{:S(2)}) copy-start(f32[512,64]{0,1:T(8,128)} %param.11) | copy-start | bytes 393220

commit v4 on v3

--- a/solution.py
+++ b/solution.py
@@ -90,28 +90,54 @@
             preferred_element_type=jnp.float32,
         )
 
+    mid = rows // 2
+
+    def load_row(signal, r):
+        return jnp.concatenate(
+            [x[r * copies + c, signal].astype(jnp.float32) for c in range(copies)], axis=0
+        )
+
     def widen(signal):
+        wide[0] = load_row(signal, 0)
+        wide[mid] = load_row(signal, mid)
+
         def one_row(r, carry):
-            for c in range(copies):
-                wide[r, c * part : (c + 1) * part] = x[r * copies + c, signal].astype(jnp.float32)
+            left, right = load_row(signal, r), load_row(signal, rows - r)
+            wide[r] = left + right
+            wide[mid + r] = left - right
             return carry
 
-        lax.fori_loop(0, rows, one_row, 0)
-
-    def spectrum(k):
+        lax.fori_loop(1, mid, one_row, 0)
+
+    def spectrum(k, odd):
         def add(r, sums):
-            value = wide[r]
-            return (sums[0] + one[2 * k, r] * value, sums[1] + one[2 * k + 1, r] * value)
-
-        zero = jnp.zeros((cols, width), jnp.float32)
-        g = lax.fori_loop(0, rows, add, (zero, zero), unroll=min(rows, 16))
+            plus, minus = wide[r], wide[mid + r]
+            a, b = (minus, plus) if odd else (plus, minus)
+            return (sums[0] + one[2 * k, r] * a, sums[1] + one[2 * k + 1, r] * b)
+
+        first = one[2 * k, 0] * wide[0]
+        middle_row = wide[mid]
+        if odd:
+            start = (first, one[2 * k + 1, mid] * middle_row)
+        else:
+            start = (first + one[2 * k, mid] * middle_row, jnp.zeros((cols, width), jnp.float32))
+        if mid <= 16:
+            g = start
+            for r in range(1, mid):
+                g = add(r, g)
+        else:
+            g = lax.fori_loop(1, mid, add, start)
         g = jnp.concatenate(g, axis=1).astype(jnp.bfloat16)
         return jnp.dot(g, two[k], preferred_element_type=jnp.float32)
 
+    def over_freq(step):
+        lax.fori_loop(0, mid + 1, lambda j, carry: step(2 * j, False, carry), 0)
+        lax.fori_loop(0, mid, lambda j, carry: step(2 * j + 1, True, carry), 0)
+
     widen(0)
 
-    def out_step(k, carry):
-        s = spectrum(k)
+    def out_step(k, odd, carry):
+        s = spectrum(k, odd)
         spec[k] = s
         kk = kern[k]
         if own_ch % 8 == 0:
@@ -121,25 +147,40 @@
         back[k] = nt_dot(prod.astype(jnp.bfloat16), two[k])
         return carry
 
-    lax.fori_loop(0, half, out_step, 0)
+    over_freq(out_step)
+
+    def conv_parts(r, c):
+        def add(k, sums):
+            value = back[k, c * part : (c + 1) * part]
+            return (
+                sums[0] + back_one[2 * k, r] * value[:, :width],
+                sums[1] + back_one[2 * k + 1, r] * value[:, width:],
+            )
+
+        zero = jnp.zeros((part, width), jnp.float32)
+        if half < 20:
+            even, odd = (zero, zero), (zero, zero)
+            for k in range(0, half, 2):
+                even = add(k, even)
+            for k in range(1, half, 2):
+                odd = add(k, odd)
+        else:
+            even = lax.fori_loop(0, mid + 1, lambda j, v: add(2 * j, v), (zero, zero))
+            odd = lax.fori_loop(0, mid, lambda j, v: add(2 * j + 1, v), (zero, zero))
+        return even[0] + odd[1], odd[0] + even[1]
 
     def conv_step(r, carry):
-        def add(k, total):
-            value = back[k]
-            return (
-                total + back_one[2 * k, r] * value[:, :width]
-                + back_one[2 * k + 1, r] * value[:, width:]
-            )
-
-        total = lax.fori_loop(
-            0, half, add, jnp.zeros((cols, width), jnp.float32), unroll=half if half < 20 else 1
-        )
-        total = total.astype(jnp.bfloat16)
         for c in range(copies):
-            conv[r * copies + c] = total[c * part : (c + 1) * part]
-        return carry
-
-    lax.fori_loop(0, rows, conv_step, 0)
+            keep_part, flip_part = conv_parts(r, c)
+            conv[r * copies + c] = (keep_part + flip_part).astype(jnp.bfloat16)
+            conv[(rows - r) * copies + c] = (keep_part - flip_part).astype(jnp.bfloat16)
+        return carry
+
+    for r in (0, mid):
+        for c in range(copies):
+            keep_part, flip_part = conv_parts(r, c)
+            conv[r * copies + c] = (keep_part + flip_part).astype(jnp.bfloat16)
+    lax.fori_loop(1, mid, conv_step, 0)
     pl.semaphore_wait(barrier, devices - 1)
 
     def send_conv(d, carry):
@@ -161,27 +202,21 @@
     passed[...] = jnp.zeros_like(passed)
 
     def pass_step(r, carry):
-        passed[...] += jnp.concatenate(
-            [
-                x[r * copies + c, 1].astype(jnp.float32) * wide[r, c * part : (c + 1) * part]
-                for c in range(copies)
-            ],
-            axis=0,
-        )
+        passed[...] += load_row(0, r) * load_row(1, r)
         return carry
 
     lax.fori_loop(0, rows, pass_step, 0)
     widen(1)
 
-    def in_step(k, carry):
-        s = spectrum(k)
+    def in_step(k, odd, carry):
+        s = spectrum(k, odd)
         o = spec[k]
         ir, ii, outr, outi = s[:, :width], s[:, width:], o[:, :width], o[:, width:]
         cross = jnp.concatenate([outr * ir + outi * ii, outi * ir - outr * ii], axis=1)
         corr_part[k] = split_dot(over_batch(cross), two[k])
         return carry
 
-    lax.fori_loop(0, half, in_step, 0)
+    over_freq(in_step)
 
     def corr_step(r, carry):
         def add(k, total):
@@ -213,26 +248,44 @@
     lane = lax.broadcasted_iota(jnp.int32, (own_ch, width), 1)
     pay[:, 4 * states :] = jnp.where(lane == 0, corr[0], products)
 
+    row, copy = lax.axis_index("seq"), lax.axis_index("batch")
+
     def send_sums(d, carry):
-        to = (me + d) % devices
         pltpu.make_async_remote_copy(
             src_ref=pay,
-            dst_ref=sums_out.at[me],
+            dst_ref=sums_out.at[copy, row],
             send_sem=sems.at[0],
             recv_sem=sems.at[1],
-            device_id=peer_of(to, copies),
+            device_id={"seq": (row + d) % rows, "batch": copy},
             device_id_type=pl.DeviceIdType.MESH,
         ).start()
         return carry
 
-    lax.fori_loop(1, devices, send_sums, 0)
-    sums_out[me] = pay[...]
+    lax.fori_loop(1, rows, send_sums, 0)
+    sums_out[copy, row] = pay[...]
+    slots = sums_out.at[0, pl.ds(0, rows - 1)]
+    pltpu.make_async_copy(slots, slots, sems.at[1]).wait()
+
+    def forward_sums(d, carry):
+        pltpu.make_async_remote_copy(
+            src_ref=sums_out.at[copy],
+            dst_ref=sums_out.at[copy],
+            send_sem=sems.at[5],
+            recv_sem=sems.at[6],
+            device_id={"seq": row, "batch": (copy + d) % copies},
+            device_id_type=pl.DeviceIdType.MESH,
+        ).start()
+        return carry
+
+    lax.fori_loop(1, copies, forward_sums, 0)
     keep.wait()
     others = pl.ds(0, devices - 1)
     for sem in (2, 3):
         pltpu.make_async_copy(conv_out.at[others], conv_out.at[others], sems.at[sem]).wait()
-    for sem in (0, 1):
-        pltpu.make_async_copy(sums_out.at[others], sums_out.at[others], sems.at[sem]).wait()
+    pltpu.make_async_copy(slots, slots, sems.at[0]).wait()
+    groups = sums_out.at[pl.ds(0, copies - 1)]
+    for sem in (5, 6):
+        pltpu.make_async_copy(groups, groups, sems.at[sem]).wait()
 
 
 def middle(copies, own_ch, one, back_one, corr_one, x, kern, two, fine, coarse):
@@ -248,7 +301,7 @@
         lambda *refs: middle_kernel(copies, own_ch, *refs),
         out_shape=(
             jax.ShapeDtypeStruct((devices, part, width), jnp.bfloat16),
-            jax.ShapeDtypeStruct((devices, own_ch, lanes), f32),
+            jax.ShapeDtypeStruct((copies, rows, own_ch, lanes), f32),
         ),
         in_specs=[smem] * 3 + [vmem] * 5,
         out_specs=[vmem] * 2,
@@ -261,7 +314,7 @@
             pltpu.VMEM((2 * rows, own_ch, width), f32),
             pltpu.VMEM((cols, width), f32),
             pltpu.VMEM((own_ch, lanes), f32),
-            pltpu.SemaphoreType.DMA((5,)),
+            pltpu.SemaphoreType.DMA((7,)),
         ],
         compiler_params=pltpu.CompilerParams(
             collective_id=0, has_side_effects=True, vmem_limit_bytes=52 * 1024 * 1024
@@ -356,7 +409,7 @@
         fine.astype(jnp.bfloat16),
         jnp.concatenate([coarse, coarse], axis=3),
     )
-    packed = packed.reshape(channels, -1)
+    packed = jnp.swapaxes(packed, 0, 1).reshape(channels, -1)
     conv = conv.reshape(devices, batch_rows, own_ch, slice_len)
     conv = conv.transpose(1, 3, 0, 2).reshape(batch_rows, slice_len, channels)
     input_grad = (conv.astype(jnp.float32) + passthrough * out_grad.astype(jnp.float32)).astype(

time: 87.9 us -> 78.8 us (0.90)
  Pallas kernels: 45.2 us -> 36.5 us
    pallas_call x1, Pallas kernels: 45.2 us -> 36.5 us  [middle(): pl.pallas_call(lambda *refs: middle_kernel(copies, own_ch, *refs), out_sh...]
    slice x1, local copies, waits for them, and re-layouts: 1.47 us -> 0.2 us  [local(): t1 = (packed[:, 2 * states:3 * states], packed[:, 3 * states:4 * states])]
    transpose x0 -> x1, local copies, waits for them, and re-layouts: none -> 1.21 us  [local(): packed = jnp.swapaxes(packed, 0, 1).reshape(channels, -1)]
    unnamed x63 -> x59, local copies, waits for them, and re-layouts: 5.01 us -> 4.19 us
  transfers between devices with their start and end apart: 1 -> 1, of which waited for: 1 -> 1; matrix products, arithmetic and copies ran while one was open for 25% -> 28% of each run, Pallas kernels for 0% -> 0%
where the time goes in v4:
time: 78.8 us; the launch traced here: 78.3 us
  Pallas kernels  36.5 us (46%)
  other arithmetic  20.4 us (26%)
  local copies, waits for them, and re-layouts  11 us (14%)
  starting transfers between devices  6.28 us (8%)
  matrix products  2.15 us (3%)
  between operations  1.09 us (1%)
  waiting for transfers between devices  0.89 us (1%)
    pallas_call x1, Pallas kernels, middle(): pl.pallas_call(lambda *refs: middle_kernel(copies, own_ch, *refs), out_sh...  36.5 us
    all_to_all x1, starting transfers between devices, local(): both = lax.all_to_all(both, AXES, split_axis=0, concat_axis=0, tiled=True)  6.28 us
    unnamed x59, local copies, waits for them, and re-layouts  4.19 us
    another operation x1, other arithmetic  3.12 us
    squeeze x2, local copies, waits for them, and re-layouts, local(): lam = (fine[0][..., 1], fine[1][..., 1])  2.18 us
    mul x1, other arithmetic, local(): -2.0 * shrink * h[1]  1.89 us
    convert_element_type x1, other arithmetic, local(): table_two.astype(jnp.bfloat16)  1.65 us
    sin x2, other arithmetic, cos_sin(): return (jnp.cos(phases), jnp.sin(phases))  1.6 us
  transfers between devices with their start and end apart: 1, of which 1 were waited for; matrix products, arithmetic and copies ran while one was open for 28% of the time, Pallas kernels for 0%

profile of v4, /device:TPU:15, one launch (start us, length us, event | category | flops | bytes accessed | tf_op | source)
XLA Modules:
  0.0 78.3 jit_solution(12861671026822407377)
XLA Ops:
  0.6 1.4 %copy.117 = bf16[4,128,512]{1,2,0:T(8,128)(2,1)S(1)} copy(bf16[4,128,512]{2,1,0:T(8,128)(2,1)} %param.8) | data formatting | bytes 1048576 | tf_op args[1]
  2.1 0.3 copy.119
  2.4 1.1 %pad_maximum_fusion = bf16[32,2,64,128]{3,2,1,0:T(8,128)(2,1)} fusion(bf16[32,1,64,128]{3,2,1,0:T(8,128)(2,1)S(1)} %bitcast.75, bf16[32,1,64,128]{3,2,1,0:T(8,128)(2,1)S(1)} %bitcast.74), kind=kLoop, calls=%fused_computation.9 | loop fusion | flops 524288 | bytes 2097152 | tf_op jit(solution)/shard_map/concatenate | solution.py:342
  3.5 6.3 %all-to-all-start = ((bf16[32,2,64,128]{3,2,1,0:T(8,128)(2,1)}), bf16[32,2,64,128]{3,2,1,0:T(8,128)(2,1)S(1)}, u32[]{:S(2)}, u32[]{:S(2)}) async-start(bf16[32,2,64,128]{3,2,1,0:T(8,128)(2,1)} %pad_maximum_fusion), calls=%async_computation | async-start | bytes 2097152 | tf_op jit(solution)/shard_map/all_to_all | solution.py:343
  9.8 0.7 sine_negate_fusion
  10.5 0.9 %fusion.37 = (f32[128,128]{1,0:T(8,128)}, f32[128,128]{1,0:T(8,128)}) fusion(), kind=kLoop, calls=%fused_computation.97 | loop fusion | flops 229376 | bytes 131072 | tf_op jit(solution)/shard_map/sin | solution.py:17
  11.4 0.7 fusion.53
  12.1 0.8 negate_sqrt_fusion
  12.9 0.8 %multiply_subtract_fusion.6 = (f32[16,64]{0,1:T(8,128)S(1)}, f32[16,64]{0,1:T(8,128)S(1)}) fusion(f32[512,64]{0,1:T(8,128)} %param.10, s32[]{:T(128)S(6)} %select_n.80, f32[512,64]{0,1:T(8,128)S(1)} %get-tuple-element.74), kind=kLoop, calls=%fused_computation.109 | loop fusion | flops 7168 | bytes 16388 | tf_op jit(solution)/shard_map/sub | solution.py:32
  13.9 3.1 %fusion.18 = (bf16[16,64,128]{2,1,0:T(8,128)(2,1)}, bf16[16,64,128]{2,1,0:T(8,128)(2,1)}, bf16[16,64,128]{2,1,0:T(8,128)(2,1)}, bf16[16,64,128]{2,1,0:T(8,128)(2...) fusion(f32[16,64]{1,0:T(8,128)S(1)} %copy.122, f32[128]{0:T(128)S(1)} %iota_convert_fusion.1, ...), kind=kLoop, calls=%fused_computation.42 | loop fusion | flops 1310720 | bytes 2105856 | tf_op jit(solution)/shard_map/convert.3
  17.2 1.1 %copy.149 = f32[16,64,1]{0,1,2:T(8,128)} copy(f32[16,64,1]{2,1,0:T(8,128)S(1)} %slice.32) | data formatting | bytes 8192 | tf_op jit(solution)/shard_map/squeeze | solution.py:379
  18.5 1.1 %copy.150 = f32[16,64,1]{0,1,2:T(8,128)} copy(f32[16,64,1]{2,1,0:T(8,128)S(1)} %slice.33) | data formatting | bytes 8192 | tf_op jit(solution)/shard_map/squeeze | solution.py:379
  19.6 1.4 %fusion.34 = (f32[16]{0:T(128)}, f32[16,64]{0,1:T(8,128)S(1)}, f32[16,64]{0,1:T(8,128)S(1)}) fusion(f32[16,64,1]{0,1,2:T(8,128)} %copy.150, f32[16,64,1]{0,1,2:T(8,128)} %copy.149, f32[512,64]{0,1:T(8,128)} %get-tuple-element.73, s32[]{:T(128)S(6)} %select_n.80, f32[512,64]{0,1:T(8,128)S(1)} %copy-done.6, f32[512,64]{0,1:T(8,128)} %param.11), kind=kLoop, calls=%fused_computation.90 | loop fusion | flops 11248 | bytes 28740 | tf_op jit(solution)/shard_map/reduce_sum | solution.py:383
  21.0 1.0 %fusion.39 = (f32[16,64]{0,1:T(8,128)S(1)}, f32[16,64]{0,1:T(8,128)S(1)}, f32[16,64]{0,1:T(8,128)S(1)}, f32[16,64]{0,1:T(8,128)S(1)}, f32[16,64]{0,1:T(8,128)S(1)}) fusion(f32[16,64]{0,1:T(8,128)S(1)} %get-tuple-element.56, f32[16,64]{0,1:T(8,128)S(1)} %get-tuple-element.57, f32[16,64,1]{0,1,2:T(8,128)} %copy.150, f32[16,64,1]{0,1,2:T(8,128)} %copy.149, ...), kind=kLoop, calls=%fused_computation.101 | loop fusion | flops 29696 | bytes 45060 | tf_op jit(solution)/shard_map/mul | solution.py:26
  22.3 1.1 %subtract_multiply_fusion = (f32[16,64,32]{1,2,0:T(8,128)S(1)}, f32[16,64,32]{1,2,0:T(8,128)S(1)}) fusion(f32[16,64]{1,0:T(8,128)S(1)} %copy.130, f32[16,64]{1,0:T(8,128)S(1)} %copy.129, f32[32]{0:T(128)S(1)} %iota_convert_fusion, f32[16,64]{1,0:T(8,128)S(1)} %copy.128, f32[16,64]{1,0:T(8,128)S(1)} %copy.127), kind=kLoop, calls=%fused_computation.39 | loop fusion | flops 393216 | bytes 278656 | tf_op jit(solution)/shard_map/mul | solution.py:387
  23.5 0.6 convolution_bitcast_fusion.1
  24.1 0.3 convolution_bitcast_fusion
  24.6 0.9 %reshape.302 = f32[17,16,256]{2,1,0:T(8,128)} reshape(f32[17,16,2,128]{3,2,1,0:T(2,128)S(1)} %copy.131) | data formatting | bytes 557056 | tf_op jit(solution)/shard_map/reshape | solution.py:392
  25.9 1.0 %fusion.12 = (f32[16,1,32,64]{3,2,1,0:T(8,128)S(1)}, f32[16,1,32,64]{3,2,1,0:T(8,128)S(1)}) fusion(f32[16,64]{1,0:T(8,128)S(1)} %copy-done.18, f32[32]{0:T(128)S(1)} %copy-done.23, f32[16,64]{1,0:T(8,128)S(1)} %copy-done.16), kind=kLoop, calls=%fused_computation.30 | loop fusion | flops 131072 | bytes 270464 | tf_op jit(solution)/shard_map/mul | solution.py:36
  27.2 1.1 %pad_maximum_fusion.1.refs_6_ = bf16[16,256,128]{2,1,0:T(8,128)(2,1)} fusion(bf16[16,64,128]{2,1,0:T(8,128)(2,1)S(1)} %get-tuple-element.85, bf16[16,64,128]{2,1,0:T(8,128)(2,1)S(1)} %copy-done.4, bf16[16,64,128]{2,1,0:T(8,128)(2,1)S(1)} %copy-done.5, bf16[16,64,128]{2,1,0:T(8,128)(2,1)S(1)} %copy-done.3), kind=kLoop, calls=%fused_computation.13 | loop fusion | flops 4194304 | bytes 2097152 | tf_op jit(solution)/shard_map/concatenate | solution.py:398
  28.3 0.6 fusion.19
  29.0 1.6 %fusion.refs_5_ = bf16[17,256,256]{2,1,0:T(8,128)(2,1)} fusion(f32[17,128,128]{2,1,0:T(8,128)S(1)} %get-tuple-element.72, f32[17,128,128]{2,1,0:T(8,128)S(1)} %get-tuple-element.71, f32[17,128,128]{2,1,0:T(8,128)S(1)} %get-tuple-element.70), kind=kLoop, calls=%fused_computation.1 | loop fusion | flops 8912896 | bytes 5570560 | tf_op jit(solution)/shard_map/convert_element_type | solution.py:408
  30.8 1.3 %fusion.3.refs_4_ = f32[17,16,256]{2,1,0:T(8,128)S(1)} fusion(f32[17,16,256]{2,1,0:T(8,128)S(1)} %copy-done.11, f32[17,128,128]{2,1,0:T(8,128)S(1)} %get-tuple-element.72, f32[17,128,128]{2,1,0:T(8,128)S(1)} %get-tuple-element.71, f32[17,128,128]{2,1,0:T(8,128)S(1)} %get-tuple-element.70, f32[16,256]{1,0:T(8,128)S(1)} %broadcast_multiply_fusion.2), kind=kOutput, calls=%fused_computation.6 | convolution fusion | flops 110436352 | bytes 3915776 | tf_op jit(solution)/shard_map/kxa,kab->kxb/dot_general | solution.py:392
  32.0 0.9 %all-to-all-done.refs_3_ = bf16[32,2,64,128]{3,2,1,0:T(8,128)(2,1)S(1)} async-done(((bf16[32,2,64,128]{3,2,1,0:T(8,128)(2,1)}), bf16[32,2,64,128]{3,2,1,0:T(8,128)(2,1)S(1)}, u32[]{:S(2)}, u32[]{:S(2)}) %all-to-all-start) | async-done | bytes 1048608 | tf_op jit(solution)/shard_map/all_to_all | solution.py:343
  32.9 1.0 %copy-done = bf16[32,2,64,128]{3,2,1,0:T(8,128)(2,1)} copy-done((bf16[32,2,64,128]{3,2,1,0:T(8,128)(2,1)}, bf16[32,2,64,128]{3,2,1,0:T(8,128)(2,1)S(1)}, u32[]{:S(2)}) %copy-start) | copy-done | bytes 1048600
  33.9 36.5 %middle.1 = (bf16[32,64,128]{2,1,0:T(8,128)(2,1)S(1)}, f32[2,16,16,384]{3,2,1,0:T(8,128)}) custom-call(f32[34,32]{1,0:T(8,128)S(1)} %get-tuple-element.79.refs_0_, f32[34,32]{1,0:T(8,128)S(1)} %get-tuple-element.78.refs_1_, f32[34,32]{1,0:T(8,128)S(1)} %get-tuple-element.77.refs_2_, bf16[32,2,64,128]{3,2,1,0:T(8,128)(2,1)} %copy-done, ...), custom_call_target="tpu_custom_call" | custom-call | tf_op jit(solution)/shard_map/middle/pallas_call | solution.py:300
  70.4 1.2 %copy.142 = f32[16,2,16,384]{3,2,1,0:T(8,128)S(1)} copy(f32[16,2,16,384]{3,2,0,1:T(8,128)} %bitcast.76) | data formatting | bytes 1572864 | tf_op jit(solution)/shard_map/transpose | solution.py:412
  71.9 0.8 %slice_reduce_fusion = (f32[512]{0:T(512)}, f32[512]{0:T(512)S(1)}) fusion(f32[512,384]{1,0:T(8,128)S(1)} %bitcast.71), kind=kLoop, calls=%fused_computation.32 | loop fusion | bytes 8192 | tf_op jit(solution)/shard_map/slice | solution.py:446
  73.5 1.0 %copy.147 = bf16[4,128,512]{2,1,0:T(8,128)(2,1)} copy(bf16[4,128,512]{1,2,0:T(8,128)(2,1)S(1)} %fusion.7) | data formatting | bytes 1048576
  74.5 1.9 %multiply_multiply_fusion = (f32[512,64]{0,1:T(8,128)}, f32[512,64]{0,1:T(8,128)S(1)}, f32[512,64]{0,1:T(8,128)S(1)}, f32[512,64]{0,1:T(8,128)S(1)}, f32[512,64]...) fusion(f32[512,64]{0,1:T(8,128)S(1)} %copy-done.2, ...), kind=kLoop, calls=%fused_computation.44 | loop fusion | flops 1671168 | bytes 1574912 | tf_op jit(solution)/shard_map/mul | solution.py:445
  76.4 1.1 %multiply_multiply_fusion.1 = (f32[512,64]{0,1:T(8,128)}, f32[512,64]{0,1:T(8,128)S(1)}, f32[512,64]{0,1:T(8,128)}, f32[512,64]{0,1:T(8,128)S(1)}, f32[512,64]{0,1:T(8,128)S(1)}) fusion(f32[512,64]{0,1:T(8,128)S(1)} %copy-done.2, f32[512,64]{0,1:T(8,128)S(1)} %get-tuple-element.49, f32[512,64]{0,1:T(8,128)S(1)} %get-tuple-element.48, ...), kind=kLoop, calls=%fused_computation.45 | loop fusion | flops 2293760 | bytes 2361344 | tf_op jit(solution)/shard_map/mul | solution.py:444
  77.5 0.8 %subtract_multiply_fusion.1 = f32[512,64]{0,1:T(8,128)} fusion(f32[512,64]{0,1:T(8,128)S(1)} %get-tuple-element.65, f32[512,64]{0,1:T(8,128)S(1)} %get-tuple-element.64, f32[512,64]{0,1:T(8,128)S(1)} %copy-done.6, f32[512,64]{0,1:T(8,128)S(1)} %get-tuple-element.43, f32[512,64]{0,1:T(8,128)S(1)} %copy-done.7, f32[512,64]{0,1:T(8,128)S(1)} %get-tuple-element.51, ...), kind=kLoop, calls=%fused_computation.47 | loop fusion | flops 524288 | bytes 1048576 | tf_op jit(solution)/shard_map/mul | solution.py:442
  (84 shorter events, 2.8 us)
Async XLA Ops:
  0.6 1.5 %copy-start.8 = (bf16[4,128,512]{2,1,0:T(8,128)(2,1)S(1)}, bf16[4,128,512]{2,1,0:T(8,128)(2,1)}, u32[]{:S(2)}) copy-start(bf16[4,128,512]{2,1,0:T(8,128)(2,1)} %param.7) | copy-start | bytes 1572868
  2.4 9.7 %copy-start.1 = (f32[512,64]{0,1:T(8,128)S(1)}, f32[512,64]{0,1:T(8,128)}, u32[]{:S(2)}) copy-start(f32[512,64]{0,1:T(8,128)} %param.9) | copy-start | bytes 393220
  3.5 29.4 %all-to-all-start = ((bf16[32,2,64,128]{3,2,1,0:T(8,128)(2,1)}), bf16[32,2,64,128]{3,2,1,0:T(8,128)(2,1)S(1)}, u32[]{:S(2)}, u32[]{:S(2)}) async-start(bf16[32,2,64,128]{3,2,1,0:T(8,128)(2,1)} %pad_maximum_fusion), calls=%async_computation | async-start | bytes 2097152 | tf_op jit(solution)/shard_map/all_to_all | solution.py:343
  9.8 12.5 %copy-start.22 = (f32[32]{0:T(128)}, f32[32]{0:T(128)S(1)}, u32[]{:S(2)}) copy-start(f32[32]{0:T(128)S(1)} %iota_convert_fusion) | copy-start | bytes 388
  12.9 0.9 %copy-start.10 = (f32[512,64]{0,1:T(8,128)}, f32[512,64]{0,1:T(8,128)S(1)}, u32[]{:S(2)}) copy-start(f32[512,64]{0,1:T(8,128)S(1)} %get-tuple-element.74) | copy-start | bytes 393220
  17.0 2.6 %copy-start.6 = (f32[512,64]{0,1:T(8,128)S(1)}, f32[512,64]{0,1:T(8,128)}, u32[]{:S(2)}) copy-start(f32[512,64]{0,1:T(8,128)} %param.12) | copy-start | bytes 393220
  19.5 4.6 %copy-start.14 = (f32[17,1,32]{2,0,1:T(8,128)S(1)}, f32[17,1,32]{2,0,1:T(8,128)}, u32[]{:S(2)}) copy-start(f32[17,1,32]{2,0,1:T(8,128)} %get-tuple-element.89) | copy-start | bytes 6532
  22.1 1.4 %copy-start.15 = (f32[16,64]{1,0:T(8,128)}, f32[16,64]{1,0:T(8,128)S(1)}, u32[]{:S(2)}) copy-start(f32[16,64]{1,0:T(8,128)S(1)} %copy.128) | copy-start | bytes 12292
  22.2 1.3 %copy-start.17 = (f32[16,64]{1,0:T(8,128)}, f32[16,64]{1,0:T(8,128)S(1)}, u32[]{:S(2)}) copy-start(f32[16,64]{1,0:T(8,128)S(1)} %copy.129) | copy-start | bytes 12292
  24.0 1.9 %copy-start.16 = (f32[16,64]{1,0:T(8,128)S(1)}, f32[16,64]{1,0:T(8,128)}, u32[]{:S(2)}) copy-start(f32[16,64]{1,0:T(8,128)} %copy-done.15) | copy-start | bytes 12292
  24.1 1.9 %copy-start.18 = (f32[16,64]{1,0:T(8,128)S(1)}, f32[16,64]{1,0:T(8,128)}, u32[]{:S(2)}) copy-start(f32[16,64]{1,0:T(8,128)} %copy-done.17) | copy-start | bytes 12292
  24.1 1.9 %copy-start.23 = (f32[32]{0:T(128)S(1)}, f32[32]{0:T(128)}, u32[]{:S(2)}) copy-start(f32[32]{0:T(128)} %copy-done.22) | copy-start | bytes 388
  24.1 3.1 %copy-start.3 = (bf16[16,64,128]{2,1,0:T(8,128)(2,1)S(1)}, bf16[16,64,128]{2,1,0:T(8,128)(2,1)}, u32[]{:S(2)}) copy-start(bf16[16,64,128]{2,1,0:T(8,128)(2,1)} %get-tuple-element.82) | copy-start | bytes 786436
  24.1 3.1 %copy-start.4 = (bf16[16,64,128]{2,1,0:T(8,128)(2,1)S(1)}, bf16[16,64,128]{2,1,0:T(8,128)(2,1)}, u32[]{:S(2)}) copy-start(bf16[16,64,128]{2,1,0:T(8,128)(2,1)} %get-tuple-element.83) | copy-start | bytes 786436
  24.1 3.1 %copy-start.5 = (bf16[16,64,128]{2,1,0:T(8,128)(2,1)S(1)}, bf16[16,64,128]{2,1,0:T(8,128)(2,1)}, u32[]{:S(2)}) copy-start(bf16[16,64,128]{2,1,0:T(8,128)(2,1)} %get-tuple-element.84) | copy-start | bytes 786436
  25.5 2.7 %copy-start.12 = (f32[128,128]{1,0:T(8,128)S(1)}, f32[128,128]{1,0:T(8,128)}, u32[]{:S(2)}) copy-start(f32[128,128]{1,0:T(8,128)} %get-tuple-element.94) | copy-start | bytes 196612
  25.5 2.7 %copy-start.13 = (f32[128,128]{1,0:T(8,128)S(1)}, f32[128,128]{1,0:T(8,128)}, u32[]{:S(2)}) copy-start(f32[128,128]{1,0:T(8,128)} %get-tuple-element.95) | copy-start | bytes 196612
  25.5 2.7 %copy-start.19 = (f32[17,128]{1,0:T(8,128)S(1)}, f32[17,128]{1,0:T(8,128)}, u32[]{:S(2)}) copy-start(f32[17,128]{1,0:T(8,128)} %get-tuple-element.96) | copy-start | bytes 26116
  25.5 2.7 %copy-start.20 = (f32[17,128]{1,0:T(8,128)S(1)}, f32[17,128]{1,0:T(8,128)}, u32[]{:S(2)}) copy-start(f32[17,128]{1,0:T(8,128)} %get-tuple-element.97) | copy-start | bytes 26116
  28.9 1.7 %copy-start.25 = (f32[16]{0:T(128)S(1)}, f32[16]{0:T(128)}, u32[]{:S(2)}) copy-start(f32[16]{0:T(128)} %get-tuple-element.55) | copy-start | bytes 196
  28.9 1.7 %copy-start.24 = (f32[256]{0:T(256)S(1)}, f32[256]{0:T(256)}, u32[]{:S(2)}) copy-start(f32[256]{0:T(256)} %constant.109.clone.1) | copy-start | bytes 3076
  28.9 1.8 %copy-start.11 = (f32[17,16,256]{2,1,0:T(8,128)S(1)}, f32[17,16,256]{2,1,0:T(8,128)}, u32[]{:S(2)}) copy-start(f32[17,16,256]{2,1,0:T(8,128)} %reshape.302) | copy-start | bytes 835588
  32.9 1.0 %copy-start = (bf16[32,2,64,128]{3,2,1,0:T(8,128)(2,1)}, bf16[32,2,64,128]{3,2,1,0:T(8,128)(2,1)S(1)}, u32[]{:S(2)}) copy-start(bf16[32,2,64,128]{3,2,1,0:T(8,128)(2,1)S(1)} %all-to-all-done.refs_3_) | copy-start | bytes 3145732
  71.8 1.4 %copy-start.21 = (f32[512]{0:T(512)S(1)}, f32[512]{0:T(512)}, u32[]{:S(2)}) copy-start(f32[512]{0:T(512)} %param.13) | copy-start | bytes 6148
  73.1 1.4 %copy-start.2 = (f32[512,64]{0,1:T(8,128)S(1)}, f32[512,64]{0,1:T(8,128)}, u32[]{:S(2)}) copy-start(f32[512,64]{0,1:T(8,128)} %param.9) | copy-start | bytes 393220
  73.2 1.3 %copy-start.9 = (f32[512,64]{0,1:T(8,128)S(1)}, f32[512,64]{0,1:T(8,128)}, u32[]{:S(2)}) copy-start(f32[512,64]{0,1:T(8,128)} %param.10) | copy-start | bytes 393220
  73.3 3.1 %copy-start.7 = (f32[512,64]{0,1:T(8,128)S(1)}, f32[512,64]{0,1:T(8,128)}, u32[]{:S(2)}) copy-start(f32[512,64]{0,1:T(8,128)} %param.11) | copy-start | bytes 393220

commit v5 on v4

--- a/solution.py
+++ b/solution.py
@@ -131,8 +131,15 @@
         return jnp.dot(g, two[k], preferred_element_type=jnp.float32)
 
     def over_freq(step):
-        lax.fori_loop(0, mid + 1, lambda j, carry: step(2 * j, False, carry), 0)
-        lax.fori_loop(0, mid, lambda j, carry: step(2 * j + 1, True, carry), 0)
+        for odd, count in ((False, mid + 1), (True, mid)):
+            group = next(u for u in (3, 2, 1) if count % u == 0)
+
+            def several(j, carry, odd=odd, group=group):
+                for u in range(group):
+                    carry = step(2 * (group * j + u) + int(odd), odd, carry)
+                return carry
+
+            lax.fori_loop(0, count // group, several, 0)
 
     widen(0)
 

time: 78.8 us -> 76.6 us (0.972)
  Pallas kernels: 36.5 us -> 34.3 us
    pallas_call x1, Pallas kernels: 36.5 us -> 34.3 us  [middle(): pl.pallas_call(lambda *refs: middle_kernel(copies, own_ch, *refs), out_sh...]
  transfers between devices with their start and end apart: 1 -> 1, of which waited for: 1 -> 1; matrix products, arithmetic and copies ran while one was open for 28% -> 29% of each run, Pallas kernels for 0% -> 0%
where the time goes in v5:
time: 76.6 us; the launch traced here: 76.1 us
  Pallas kernels  34.3 us (45%)
  other arithmetic  20.4 us (27%)
  local copies, waits for them, and re-layouts  11 us (14%)
  starting transfers between devices  6.28 us (8%)
  matrix products  2.15 us (3%)
  between operations  1.09 us (1%)
  waiting for transfers between devices  0.89 us (1%)
    pallas_call x1, Pallas kernels, middle(): pl.pallas_call(lambda *refs: middle_kernel(copies, own_ch, *refs), out_sh...  34.3 us
    all_to_all x1, starting transfers between devices, local(): both = lax.all_to_all(both, AXES, split_axis=0, concat_axis=0, tiled=True)  6.28 us
    unnamed x59, local copies, waits for them, and re-layouts  4.19 us
    another operation x1, other arithmetic  3.12 us
    squeeze x2, local copies, waits for them, and re-layouts, local(): lam = (fine[0][..., 1], fine[1][..., 1])  2.18 us
    mul x1, other arithmetic, local(): -2.0 * shrink * h[1]  1.89 us
    convert_element_type x1, other arithmetic, local(): table_two.astype(jnp.bfloat16)  1.65 us
    sin x2, other arithmetic, cos_sin(): return (jnp.cos(phases), jnp.sin(phases))  1.6 us
  transfers between devices with their start and end apart: 1, of which 1 were waited for; matrix products, arithmetic and copies ran while one was open for 29% of the time, Pallas kernels for 0%

profile of v5, /device:TPU:15, one launch (start us, length us, event | category | flops | bytes accessed | tf_op | source)
XLA Modules:
  0.0 76.1 jit_solution(15089747299895386870)
XLA Ops:
  0.6 1.4 %copy.117 = bf16[4,128,512]{1,2,0:T(8,128)(2,1)S(1)} copy(bf16[4,128,512]{2,1,0:T(8,128)(2,1)} %param.8) | data formatting | bytes 1048576 | tf_op args[1]
  2.1 0.3 copy.119
  2.4 1.1 %pad_maximum_fusion = bf16[32,2,64,128]{3,2,1,0:T(8,128)(2,1)} fusion(bf16[32,1,64,128]{3,2,1,0:T(8,128)(2,1)S(1)} %bitcast.75, bf16[32,1,64,128]{3,2,1,0:T(8,128)(2,1)S(1)} %bitcast.74), kind=kLoop, calls=%fused_computation.9 | loop fusion | flops 524288 | bytes 2097152 | tf_op jit(solution)/shard_map/concatenate | solution.py:349
  3.5 6.3 %all-to-all-start = ((bf16[32,2,64,128]{3,2,1,0:T(8,128)(2,1)}), bf16[32,2,64,128]{3,2,1,0:T(8,128)(2,1)S(1)}, u32[]{:S(2)}, u32[]{:S(2)}) async-start(bf16[32,2,64,128]{3,2,1,0:T(8,128)(2,1)} %pad_maximum_fusion), calls=%async_computation | async-start | bytes 2097152 | tf_op jit(solution)/shard_map/all_to_all | solution.py:350
  9.8 0.7 sine_negate_fusion
  10.5 0.9 %fusion.37 = (f32[128,128]{1,0:T(8,128)}, f32[128,128]{1,0:T(8,128)}) fusion(), kind=kLoop, calls=%fused_computation.97 | loop fusion | flops 229376 | bytes 131072 | tf_op jit(solution)/shard_map/sin | solution.py:17
  11.4 0.7 fusion.53
  12.1 0.8 negate_sqrt_fusion
  12.9 0.8 %multiply_subtract_fusion.6 = (f32[16,64]{0,1:T(8,128)S(1)}, f32[16,64]{0,1:T(8,128)S(1)}) fusion(f32[512,64]{0,1:T(8,128)} %param.10, s32[]{:T(128)S(6)} %select_n.80, f32[512,64]{0,1:T(8,128)S(1)} %get-tuple-element.74), kind=kLoop, calls=%fused_computation.109 | loop fusion | flops 7168 | bytes 16388 | tf_op jit(solution)/shard_map/sub | solution.py:32
  13.9 3.1 %fusion.18 = (bf16[16,64,128]{2,1,0:T(8,128)(2,1)}, bf16[16,64,128]{2,1,0:T(8,128)(2,1)}, bf16[16,64,128]{2,1,0:T(8,128)(2,1)}, bf16[16,64,128]{2,1,0:T(8,128)(2...) fusion(f32[16,64]{1,0:T(8,128)S(1)} %copy.122, f32[128]{0:T(128)S(1)} %iota_convert_fusion.1, ...), kind=kLoop, calls=%fused_computation.42 | loop fusion | flops 1310720 | bytes 2105856 | tf_op jit(solution)/shard_map/convert.3
  17.2 1.1 %copy.149 = f32[16,64,1]{0,1,2:T(8,128)} copy(f32[16,64,1]{2,1,0:T(8,128)S(1)} %slice.32) | data formatting | bytes 8192 | tf_op jit(solution)/shard_map/squeeze | solution.py:386
  18.5 1.1 %copy.150 = f32[16,64,1]{0,1,2:T(8,128)} copy(f32[16,64,1]{2,1,0:T(8,128)S(1)} %slice.33) | data formatting | bytes 8192 | tf_op jit(solution)/shard_map/squeeze | solution.py:386
  19.6 1.4 %fusion.34 = (f32[16]{0:T(128)}, f32[16,64]{0,1:T(8,128)S(1)}, f32[16,64]{0,1:T(8,128)S(1)}) fusion(f32[16,64,1]{0,1,2:T(8,128)} %copy.150, f32[16,64,1]{0,1,2:T(8,128)} %copy.149, f32[512,64]{0,1:T(8,128)} %get-tuple-element.73, s32[]{:T(128)S(6)} %select_n.80, f32[512,64]{0,1:T(8,128)S(1)} %copy-done.6, f32[512,64]{0,1:T(8,128)} %param.11), kind=kLoop, calls=%fused_computation.90 | loop fusion | flops 11248 | bytes 28740 | tf_op jit(solution)/shard_map/reduce_sum | solution.py:390
  21.0 1.0 %fusion.39 = (f32[16,64]{0,1:T(8,128)S(1)}, f32[16,64]{0,1:T(8,128)S(1)}, f32[16,64]{0,1:T(8,128)S(1)}, f32[16,64]{0,1:T(8,128)S(1)}, f32[16,64]{0,1:T(8,128)S(1)}) fusion(f32[16,64]{0,1:T(8,128)S(1)} %get-tuple-element.56, f32[16,64]{0,1:T(8,128)S(1)} %get-tuple-element.57, f32[16,64,1]{0,1,2:T(8,128)} %copy.150, f32[16,64,1]{0,1,2:T(8,128)} %copy.149, ...), kind=kLoop, calls=%fused_computation.101 | loop fusion | flops 29696 | bytes 45060 | tf_op jit(solution)/shard_map/mul | solution.py:26
  22.3 1.1 %subtract_multiply_fusion = (f32[16,64,32]{1,2,0:T(8,128)S(1)}, f32[16,64,32]{1,2,0:T(8,128)S(1)}) fusion(f32[16,64]{1,0:T(8,128)S(1)} %copy.130, f32[16,64]{1,0:T(8,128)S(1)} %copy.129, f32[32]{0:T(128)S(1)} %iota_convert_fusion, f32[16,64]{1,0:T(8,128)S(1)} %copy.128, f32[16,64]{1,0:T(8,128)S(1)} %copy.127), kind=kLoop, calls=%fused_computation.39 | loop fusion | flops 393216 | bytes 278656 | tf_op jit(solution)/shard_map/mul | solution.py:394
  23.5 0.6 convolution_bitcast_fusion.1
  24.1 0.3 convolution_bitcast_fusion
  24.6 0.9 %reshape.302 = f32[17,16,256]{2,1,0:T(8,128)} reshape(f32[17,16,2,128]{3,2,1,0:T(2,128)S(1)} %copy.131) | data formatting | bytes 557056 | tf_op jit(solution)/shard_map/reshape | solution.py:399
  25.9 1.0 %fusion.12 = (f32[16,1,32,64]{3,2,1,0:T(8,128)S(1)}, f32[16,1,32,64]{3,2,1,0:T(8,128)S(1)}) fusion(f32[16,64]{1,0:T(8,128)S(1)} %copy-done.18, f32[32]{0:T(128)S(1)} %copy-done.23, f32[16,64]{1,0:T(8,128)S(1)} %copy-done.16), kind=kLoop, calls=%fused_computation.30 | loop fusion | flops 131072 | bytes 270464 | tf_op jit(solution)/shard_map/mul | solution.py:36
  27.2 1.1 %pad_maximum_fusion.1.refs_6_ = bf16[16,256,128]{2,1,0:T(8,128)(2,1)} fusion(bf16[16,64,128]{2,1,0:T(8,128)(2,1)S(1)} %get-tuple-element.85, bf16[16,64,128]{2,1,0:T(8,128)(2,1)S(1)} %copy-done.4, bf16[16,64,128]{2,1,0:T(8,128)(2,1)S(1)} %copy-done.5, bf16[16,64,128]{2,1,0:T(8,128)(2,1)S(1)} %copy-done.3), kind=kLoop, calls=%fused_computation.13 | loop fusion | flops 4194304 | bytes 2097152 | tf_op jit(solution)/shard_map/concatenate | solution.py:405
  28.3 0.6 fusion.19
  29.0 1.6 %fusion.refs_5_ = bf16[17,256,256]{2,1,0:T(8,128)(2,1)} fusion(f32[17,128,128]{2,1,0:T(8,128)S(1)} %get-tuple-element.72, f32[17,128,128]{2,1,0:T(8,128)S(1)} %get-tuple-element.71, f32[17,128,128]{2,1,0:T(8,128)S(1)} %get-tuple-element.70), kind=kLoop, calls=%fused_computation.1 | loop fusion | flops 8912896 | bytes 5570560 | tf_op jit(solution)/shard_map/convert_element_type | solution.py:415
  30.8 1.3 %fusion.3.refs_4_ = f32[17,16,256]{2,1,0:T(8,128)S(1)} fusion(f32[17,16,256]{2,1,0:T(8,128)S(1)} %copy-done.11, f32[17,128,128]{2,1,0:T(8,128)S(1)} %get-tuple-element.72, f32[17,128,128]{2,1,0:T(8,128)S(1)} %get-tuple-element.71, f32[17,128,128]{2,1,0:T(8,128)S(1)} %get-tuple-element.70, f32[16,256]{1,0:T(8,128)S(1)} %broadcast_multiply_fusion.2), kind=kOutput, calls=%fused_computation.6 | convolution fusion | flops 110436352 | bytes 3915776 | tf_op jit(solution)/shard_map/kxa,kab->kxb/dot_general | solution.py:399
  32.0 0.9 %all-to-all-done.refs_3_ = bf16[32,2,64,128]{3,2,1,0:T(8,128)(2,1)S(1)} async-done(((bf16[32,2,64,128]{3,2,1,0:T(8,128)(2,1)}), bf16[32,2,64,128]{3,2,1,0:T(8,128)(2,1)S(1)}, u32[]{:S(2)}, u32[]{:S(2)}) %all-to-all-start) | async-done | bytes 1048608 | tf_op jit(solution)/shard_map/all_to_all | solution.py:350
  32.9 1.0 %copy-done = bf16[32,2,64,128]{3,2,1,0:T(8,128)(2,1)} copy-done((bf16[32,2,64,128]{3,2,1,0:T(8,128)(2,1)}, bf16[32,2,64,128]{3,2,1,0:T(8,128)(2,1)S(1)}, u32[]{:S(2)}) %copy-start) | copy-done | bytes 1048600
  33.9 34.3 %middle.1 = (bf16[32,64,128]{2,1,0:T(8,128)(2,1)S(1)}, f32[2,16,16,384]{3,2,1,0:T(8,128)}) custom-call(f32[34,32]{1,0:T(8,128)S(1)} %get-tuple-element.79.refs_0_, f32[34,32]{1,0:T(8,128)S(1)} %get-tuple-element.78.refs_1_, f32[34,32]{1,0:T(8,128)S(1)} %get-tuple-element.77.refs_2_, bf16[32,2,64,128]{3,2,1,0:T(8,128)(2,1)} %copy-done, ...), custom_call_target="tpu_custom_call" | custom-call | tf_op jit(solution)/shard_map/middle/pallas_call | solution.py:307
  68.2 1.2 %copy.142 = f32[16,2,16,384]{3,2,1,0:T(8,128)S(1)} copy(f32[16,2,16,384]{3,2,0,1:T(8,128)} %bitcast.76) | data formatting | bytes 1572864 | tf_op jit(solution)/shard_map/transpose | solution.py:419
  69.6 0.8 %slice_reduce_fusion = (f32[512]{0:T(512)}, f32[512]{0:T(512)S(1)}) fusion(f32[512,384]{1,0:T(8,128)S(1)} %bitcast.71), kind=kLoop, calls=%fused_computation.32 | loop fusion | bytes 8192 | tf_op jit(solution)/shard_map/slice | solution.py:453
  71.3 1.0 %copy.147 = bf16[4,128,512]{2,1,0:T(8,128)(2,1)} copy(bf16[4,128,512]{1,2,0:T(8,128)(2,1)S(1)} %fusion.7) | data formatting | bytes 1048576
  72.3 1.9 %multiply_multiply_fusion = (f32[512,64]{0,1:T(8,128)}, f32[512,64]{0,1:T(8,128)S(1)}, f32[512,64]{0,1:T(8,128)S(1)}, f32[512,64]{0,1:T(8,128)S(1)}, f32[512,64]...) fusion(f32[512,64]{0,1:T(8,128)S(1)} %copy-done.2, ...), kind=kLoop, calls=%fused_computation.44 | loop fusion | flops 1671168 | bytes 1574912 | tf_op jit(solution)/shard_map/mul | solution.py:452
  74.2 1.1 %multiply_multiply_fusion.1 = (f32[512,64]{0,1:T(8,128)}, f32[512,64]{0,1:T(8,128)S(1)}, f32[512,64]{0,1:T(8,128)}, f32[512,64]{0,1:T(8,128)S(1)}, f32[512,64]{0,1:T(8,128)S(1)}) fusion(f32[512,64]{0,1:T(8,128)S(1)} %copy-done.2, f32[512,64]{0,1:T(8,128)S(1)} %get-tuple-element.49, f32[512,64]{0,1:T(8,128)S(1)} %get-tuple-element.48, ...), kind=kLoop, calls=%fused_computation.45 | loop fusion | flops 2293760 | bytes 2361344 | tf_op jit(solution)/shard_map/mul | solution.py:451
  75.2 0.8 %subtract_multiply_fusion.1 = f32[512,64]{0,1:T(8,128)} fusion(f32[512,64]{0,1:T(8,128)S(1)} %get-tuple-element.65, f32[512,64]{0,1:T(8,128)S(1)} %get-tuple-element.64, f32[512,64]{0,1:T(8,128)S(1)} %copy-done.6, f32[512,64]{0,1:T(8,128)S(1)} %get-tuple-element.43, f32[512,64]{0,1:T(8,128)S(1)} %copy-done.7, f32[512,64]{0,1:T(8,128)S(1)} %get-tuple-element.51, ...), kind=kLoop, calls=%fused_computation.47 | loop fusion | flops 524288 | bytes 1048576 | tf_op jit(solution)/shard_map/mul | solution.py:449
  (84 shorter events, 2.8 us)
Async XLA Ops:
  0.6 1.5 %copy-start.8 = (bf16[4,128,512]{2,1,0:T(8,128)(2,1)S(1)}, bf16[4,128,512]{2,1,0:T(8,128)(2,1)}, u32[]{:S(2)}) copy-start(bf16[4,128,512]{2,1,0:T(8,128)(2,1)} %param.7) | copy-start | bytes 1572868
  2.4 9.7 %copy-start.1 = (f32[512,64]{0,1:T(8,128)S(1)}, f32[512,64]{0,1:T(8,128)}, u32[]{:S(2)}) copy-start(f32[512,64]{0,1:T(8,128)} %param.9) | copy-start | bytes 393220
  3.5 29.4 %all-to-all-start = ((bf16[32,2,64,128]{3,2,1,0:T(8,128)(2,1)}), bf16[32,2,64,128]{3,2,1,0:T(8,128)(2,1)S(1)}, u32[]{:S(2)}, u32[]{:S(2)}) async-start(bf16[32,2,64,128]{3,2,1,0:T(8,128)(2,1)} %pad_maximum_fusion), calls=%async_computation | async-start | bytes 2097152 | tf_op jit(solution)/shard_map/all_to_all | solution.py:350
  9.8 12.5 %copy-start.22 = (f32[32]{0:T(128)}, f32[32]{0:T(128)S(1)}, u32[]{:S(2)}) copy-start(f32[32]{0:T(128)S(1)} %iota_convert_fusion) | copy-start | bytes 388
  12.9 0.9 %copy-start.10 = (f32[512,64]{0,1:T(8,128)}, f32[512,64]{0,1:T(8,128)S(1)}, u32[]{:S(2)}) copy-start(f32[512,64]{0,1:T(8,128)S(1)} %get-tuple-element.74) | copy-start | bytes 393220
  17.0 2.6 %copy-start.6 = (f32[512,64]{0,1:T(8,128)S(1)}, f32[512,64]{0,1:T(8,128)}, u32[]{:S(2)}) copy-start(f32[512,64]{0,1:T(8,128)} %param.12) | copy-start | bytes 393220
  19.5 4.6 %copy-start.14 = (f32[17,1,32]{2,0,1:T(8,128)S(1)}, f32[17,1,32]{2,0,1:T(8,128)}, u32[]{:S(2)}) copy-start(f32[17,1,32]{2,0,1:T(8,128)} %get-tuple-element.89) | copy-start | bytes 6532
  22.1 1.4 %copy-start.15 = (f32[16,64]{1,0:T(8,128)}, f32[16,64]{1,0:T(8,128)S(1)}, u32[]{:S(2)}) copy-start(f32[16,64]{1,0:T(8,128)S(1)} %copy.128) | copy-start | bytes 12292
  22.2 1.3 %copy-start.17 = (f32[16,64]{1,0:T(8,128)}, f32[16,64]{1,0:T(8,128)S(1)}, u32[]{:S(2)}) copy-start(f32[16,64]{1,0:T(8,128)S(1)} %copy.129) | copy-start | bytes 12292
  24.0 1.9 %copy-start.16 = (f32[16,64]{1,0:T(8,128)S(1)}, f32[16,64]{1,0:T(8,128)}, u32[]{:S(2)}) copy-start(f32[16,64]{1,0:T(8,128)} %copy-done.15) | copy-start | bytes 12292
  24.1 1.9 %copy-start.18 = (f32[16,64]{1,0:T(8,128)S(1)}, f32[16,64]{1,0:T(8,128)}, u32[]{:S(2)}) copy-start(f32[16,64]{1,0:T(8,128)} %copy-done.17) | copy-start | bytes 12292
  24.1 1.9 %copy-start.23 = (f32[32]{0:T(128)S(1)}, f32[32]{0:T(128)}, u32[]{:S(2)}) copy-start(f32[32]{0:T(128)} %copy-done.22) | copy-start | bytes 388
  24.1 3.1 %copy-start.3 = (bf16[16,64,128]{2,1,0:T(8,128)(2,1)S(1)}, bf16[16,64,128]{2,1,0:T(8,128)(2,1)}, u32[]{:S(2)}) copy-start(bf16[16,64,128]{2,1,0:T(8,128)(2,1)} %get-tuple-element.82) | copy-start | bytes 786436
  24.1 3.1 %copy-start.4 = (bf16[16,64,128]{2,1,0:T(8,128)(2,1)S(1)}, bf16[16,64,128]{2,1,0:T(8,128)(2,1)}, u32[]{:S(2)}) copy-start(bf16[16,64,128]{2,1,0:T(8,128)(2,1)} %get-tuple-element.83) | copy-start | bytes 786436
  24.1 3.1 %copy-start.5 = (bf16[16,64,128]{2,1,0:T(8,128)(2,1)S(1)}, bf16[16,64,128]{2,1,0:T(8,128)(2,1)}, u32[]{:S(2)}) copy-start(bf16[16,64,128]{2,1,0:T(8,128)(2,1)} %get-tuple-element.84) | copy-start | bytes 786436
  25.5 2.7 %copy-start.12 = (f32[128,128]{1,0:T(8,128)S(1)}, f32[128,128]{1,0:T(8,128)}, u32[]{:S(2)}) copy-start(f32[128,128]{1,0:T(8,128)} %get-tuple-element.94) | copy-start | bytes 196612
  25.5 2.7 %copy-start.13 = (f32[128,128]{1,0:T(8,128)S(1)}, f32[128,128]{1,0:T(8,128)}, u32[]{:S(2)}) copy-start(f32[128,128]{1,0:T(8,128)} %get-tuple-element.95) | copy-start | bytes 196612
  25.5 2.7 %copy-start.19 = (f32[17,128]{1,0:T(8,128)S(1)}, f32[17,128]{1,0:T(8,128)}, u32[]{:S(2)}) copy-start(f32[17,128]{1,0:T(8,128)} %get-tuple-element.96) | copy-start | bytes 26116
  25.5 2.7 %copy-start.20 = (f32[17,128]{1,0:T(8,128)S(1)}, f32[17,128]{1,0:T(8,128)}, u32[]{:S(2)}) copy-start(f32[17,128]{1,0:T(8,128)} %get-tuple-element.97) | copy-start | bytes 26116
  28.9 1.7 %copy-start.25 = (f32[16]{0:T(128)S(1)}, f32[16]{0:T(128)}, u32[]{:S(2)}) copy-start(f32[16]{0:T(128)} %get-tuple-element.55) | copy-start | bytes 196
  28.9 1.7 %copy-start.24 = (f32[256]{0:T(256)S(1)}, f32[256]{0:T(256)}, u32[]{:S(2)}) copy-start(f32[256]{0:T(256)} %constant.109.clone.1) | copy-start | bytes 3076
  28.9 1.8 %copy-start.11 = (f32[17,16,256]{2,1,0:T(8,128)S(1)}, f32[17,16,256]{2,1,0:T(8,128)}, u32[]{:S(2)}) copy-start(f32[17,16,256]{2,1,0:T(8,128)} %reshape.302) | copy-start | bytes 835588
  32.9 1.0 %copy-start = (bf16[32,2,64,128]{3,2,1,0:T(8,128)(2,1)}, bf16[32,2,64,128]{3,2,1,0:T(8,128)(2,1)S(1)}, u32[]{:S(2)}) copy-start(bf16[32,2,64,128]{3,2,1,0:T(8,128)(2,1)S(1)} %all-to-all-done.refs_3_) | copy-start | bytes 3145732
  69.6 1.4 %copy-start.21 = (f32[512]{0:T(512)S(1)}, f32[512]{0:T(512)}, u32[]{:S(2)}) copy-start(f32[512]{0:T(512)} %param.13) | copy-start | bytes 6148
  70.9 1.4 %copy-start.2 = (f32[512,64]{0,1:T(8,128)S(1)}, f32[512,64]{0,1:T(8,128)}, u32[]{:S(2)}) copy-start(f32[512,64]{0,1:T(8,128)} %param.9) | copy-start | bytes 393220
  70.9 1.3 %copy-start.9 = (f32[512,64]{0,1:T(8,128)S(1)}, f32[512,64]{0,1:T(8,128)}, u32[]{:S(2)}) copy-start(f32[512,64]{0,1:T(8,128)} %param.10) | copy-start | bytes 393220
  71.0 3.1 %copy-start.7 = (f32[512,64]{0,1:T(8,128)S(1)}, f32[512,64]{0,1:T(8,128)}, u32[]{:S(2)}) copy-start(f32[512,64]{0,1:T(8,128)} %param.11) | copy-start | bytes 393220
